TPU v7x, 32 devices: a whole 2x2x4 slice. The times are simulated.
32 devices in a mesh: lat: 2 (over core), lon: 16 (over z, y, x).
Axes of the slice: x: 2, y: 2, z: 4, core: 2. Of those that a mesh axis runs over, the one named last changes fastest.
Arguments:
- features: bfloat16 [32, 128, 256], P('lat', 'lon'), may hold values from -6 to 6
- cotangent: bfloat16 [32, 128, 256], P('lat', 'lon'), may hold values from -6 to 6
- weights: bfloat16 [8, 256, 256], replicated, may hold values from -0.375 to 0.375
- basis: bfloat16 [8, 32, 3, 5], P(None, 'lat'), may hold values from -1.5 to 1.5
- polar_kernel: float32 [8, 2, 2, 2, 128], replicated, may hold values from -0.375 to 0.375
- lon_reach: int32 [32], P('lat'), may hold values from 0 to 2
Outputs:
- grad_features: bfloat16 [32, 128, 256], P('lat', 'lon')
- grad_weights: float32 [8, 256, 256], P('lat')
All inputs are finite; a program needn't handle non-finite values.
Results may differ from a plain program's by a relative error of at most 0.0049.
Values may be sent and summed in bfloat16 or wider, within the bound.
A program may use at most 64 MiB of HBM per device.

v0:
```python
import jax
import jax.numpy as jnp
from jax import lax
from jax.sharding import PartitionSpec as P

RADIUS = 1
REACH = 2
POLAR = 2


def padded(cells, sides, width, closed):
    for axis, dim in sides:
        count = lax.axis_size(axis)
        ends = count if closed else count - 1
        head = lax.slice_in_dim(cells, 0, width, axis=dim)
        tail = lax.slice_in_dim(cells, cells.shape[dim] - width, cells.shape[dim], axis=dim)
        cells = jnp.concatenate(
            [
                lax.ppermute(tail, axis, [(i, (i + 1) % count) for i in range(ends)]),
                cells,
                lax.ppermute(head, axis, [((i + 1) % count, i) for i in range(ends)]),
            ],
            axis=dim,
        )
    return cells


def from_behind(block, axis, distance):
    devices = range(lax.axis_size(axis))
    route = [((i - distance) % len(devices), i) for i in devices]
    return lax.ppermute(block, axis, route)


def on_device(features, cotangent, weights, basis, polar_kernel, lon_reach):
    lat_rows, lon_cols, channels = features.shape
    kernels = weights.shape[0]
    lat_count = lax.axis_size("lat")
    lon_count = lax.axis_size("lon")
    lat_index = lax.axis_index("lat")
    lon_index = lax.axis_index("lon")
    at_north = lat_index == 0
    at_south = lat_index == lat_count - 1
    at_pole = jnp.logical_or(at_north, at_south)
    lon_total = lon_cols * lon_count
    own_cols = lon_index * lon_cols + jnp.arange(lon_cols, dtype=jnp.int32)
    offsets = jnp.abs(jnp.arange(2 * REACH + 1, dtype=jnp.int32) - REACH)
    reach_mask = (offsets[None, :] <= lon_reach[:, None]).astype(basis.dtype)
    masked = basis * reach_mask[None, :, None, :]
    neighbours = padded(features, (("lat", 0),), RADIUS, False)
    partner_rows = from_behind(
        (features[:RADIUS], features[lat_rows - RADIUS :]), "lon", lon_count // 2
    )
    upper_rows = jnp.where(at_north, partner_rows[0][::-1], neighbours[:RADIUS])
    lower_rows = jnp.where(at_south, partner_rows[1][::-1], neighbours[lat_rows + RADIUS :])
    lengthened = jnp.concatenate([upper_rows, features, lower_rows], 0)
    widened = padded(lengthened, (("lon", 1),), REACH, True)
    basis_sum = jnp.zeros((kernels, lat_rows, lon_cols, channels), jnp.float32)
    for row_off in range(2 * RADIUS + 1):
        windows = jnp.stack(
            [
                widened[row_off : row_off + lat_rows, col_off : col_off + lon_cols]
                for col_off in range(2 * REACH + 1)
            ],
            1,
        )
        basis_sum = basis_sum + jnp.einsum(
            "kib,ibjc->kijc", masked[:, :, row_off], windows, preferred_element_type=jnp.float32
        )
    hemisphere = jnp.where(at_north, polar_kernel[:, 0], polar_kernel[:, 1])
    polar_in = jnp.where(at_north, features[:POLAR], features[lat_rows - POLAR :])
    polar_zero = jnp.zeros((kernels, POLAR, lon_cols, channels), jnp.float32)
    block_rows = lax.all_gather(polar_in, "lon", axis=1, tiled=True)

    def compute():
        source = jnp.arange(block_rows.shape[1], dtype=jnp.int32)
        offset_idx = (source[:, None] - own_cols[None, :]) % lon_total
        circulant = jnp.take(hemisphere, offset_idx, axis=3)
        return jnp.einsum(
            "kabuj,buc->kajc",
            circulant,
            block_rows.astype(jnp.float32),
            precision=lax.Precision.HIGHEST,
        )

    polar_out = lax.cond(at_pole, compute, lambda: polar_zero)
    basis_sum = basis_sum.at[:, :POLAR].add(jnp.where(at_north, polar_out, 0.0))
    basis_sum = basis_sum.at[:, lat_rows - POLAR :].add(jnp.where(at_south, polar_out, 0.0))
    contracted = basis_sum.astype(jnp.bfloat16)
    band_grad = lax.psum_scatter(
        jnp.einsum("kijc,ijo->kco", contracted, cotangent, preferred_element_type=jnp.float32),
        "lat",
        scatter_dimension=0,
        tiled=True,
    )
    grad_weights = lax.psum(band_grad, "lon")
    grad_basis = jnp.einsum(
        "kco,ijo->kijc", weights, cotangent, preferred_element_type=jnp.float32
    ).astype(jnp.bfloat16)
    grad_wide = jnp.zeros((lat_rows + 2 * RADIUS, lon_cols + 2 * REACH, channels), jnp.float32)
    for row_off in range(2 * RADIUS + 1):
        grad_win = jnp.einsum(
            "kib,kijc->ibjc", masked[:, :, row_off], grad_basis, preferred_element_type=jnp.float32
        )
        for col_off in range(2 * REACH + 1):
            grad_wide = grad_wide.at[
                row_off : row_off + lat_rows, col_off : col_off + lon_cols
            ].add(grad_win[:, col_off])
    lon_rims = jnp.concatenate([grad_wide[:, :REACH], grad_wide[:, lon_cols + REACH :]], 1)
    beside_all = padded(lon_rims, (("lon", 1),), REACH, True)
    folded = grad_wide[:, REACH : lon_cols + REACH]
    folded = folded.at[:, :REACH].add(beside_all[:, :REACH])
    folded = folded.at[:, lon_cols - REACH :].add(beside_all[:, 3 * REACH :])
    ghosts = jnp.concatenate([folded[:RADIUS], folded[lat_rows + RADIUS :]], 0)
    beside = padded(ghosts, (("lat", 0),), RADIUS, False)
    turned = from_behind((folded[:RADIUS], folded[lat_rows + RADIUS :]), "lon", lon_count // 2)
    interior = folded[RADIUS : lat_rows + RADIUS]
    from_above = jnp.where(at_north, turned[0][::-1], beside[:RADIUS])
    from_below = jnp.where(at_south, turned[1][::-1], beside[3 * RADIUS :])
    interior = interior.at[:RADIUS].add(from_above)
    interior = interior.at[lat_rows - RADIUS :].add(from_below)
    polar_cot = jnp.where(at_north, cotangent[:POLAR], cotangent[lat_rows - POLAR :])
    running = jnp.zeros((POLAR, lon_cols, channels), jnp.float32)
    add_block_rows = lax.all_gather(polar_cot, "lon", axis=1, tiled=True)

    def compute():
        source = jnp.arange(add_block_rows.shape[1], dtype=jnp.int32)
        offset_idx = (own_cols[None, :] - source[:, None]) % lon_total
        circulant = jnp.take(hemisphere, offset_idx, axis=3)
        block_grad = jnp.einsum(
            "kco,auo->kauc", weights, add_block_rows, preferred_element_type=jnp.float32
        ).astype(jnp.bfloat16)
        return jnp.einsum(
            "kabuj,kauc->bjc",
            circulant,
            block_grad.astype(jnp.float32),
            precision=lax.Precision.HIGHEST,
        )

    polar_grad = lax.cond(at_pole, compute, lambda: running)
    interior = interior.at[:POLAR].add(jnp.where(at_north, polar_grad, 0.0))
    interior = interior.at[lat_rows - POLAR :].add(jnp.where(at_south, polar_grad, 0.0))
    return (interior.astype(jnp.bfloat16), grad_weights)


def solution(mesh):
    in_specs = (
        P("lat", "lon", None),
        P("lat", "lon", None),
        P(),
        P(None, "lat", None, None),
        P(),
        P("lat"),
    )
    out_specs = (P("lat", "lon", None), P("lat", None, None))
    return jax.shard_map(
        on_device, mesh=mesh, in_specs=in_specs, out_specs=out_specs, check_vma=False
    )
```

profile of v0, /device:TPU:0, one launch (start us, length us, event | category | flops | bytes accessed | tf_op | source)
XLA Modules:
  0.0 264.0 jit_solution(11226172266788050893)
XLA Ops:
  7.2 0.7 fusion.57
  7.9 2.3 collective-permute-start.7
  10.3 3.5 %collective-permute-start.8 = (bf16[1,8,256]{2,1,0:T(8,128)(2,1)S(1)}, bf16[1,8,256]{2,1,0:T(8,128)(2,1)S(1)}, u32[]{:S(2)}, u32[]{:S(2)}) collective-permute-start(bf16[1,8,256]{2,1,0:T(8,128)(2,1)S(1)} %get-tuple-element.348), channel_id=1, source_target_pairs={{8,0},{9,1},{10,2},{11,3},{12,4},{13,5},{14,6},{15,7},{0,8},{1,9},... | collective-permute-start | bytes 12296 | tf_op jit(solution)/shard_map/ppermute | solution.py:31
  13.8 1.3 collective-permute-start.9
  15.2 0.9 copy.489
  16.0 0.7 fusion.58
  17.1 0.7 slice_select_fusion
  17.8 0.7 compare_convert_fusion
  18.7 1.7 fusion.27
  20.7 0.5 fusion.54
  21.2 0.6 fusion.62
  21.8 0.6 fusion.61
  22.4 0.6 fusion.60
  23.0 0.7 fusion.59
  23.7 1.3 fusion.40
  25.0 1.5 scatter-add.79
  26.6 0.8 and_reduce_fusion
  27.3 1.9 add_select_fusion.4
  29.3 1.5 scatter-add.80
  30.8 1.9 add_select_fusion.3
  32.7 1.4 scatter-add.81
  34.3 2.0 add_select_fusion.2
  36.3 44.2 %all_gather.7 = bf16[2,128,256]{2,1,0:T(8,128)(2,1)} all-gather(bf16[2,8,256]{2,1,0:T(8,128)(2,1)S(1)} %slice_select_fusion), channel_id=1, replica_groups=mesh['lat'=2,'lon'=16] {'lon'}, dimensions={1}, use_global_device_ids=true | all-gather | bytes 139264 | tf_op jit(solution)/shard_map/all_gather | solution.py:72
  80.5 0.8 copy.517
  81.3 1.6 scatter-add.84
  82.9 15.0 %conditional.3 = (f32[8,2,8,256]{3,0,2,1:T(8,128)S(1)}) conditional(s32[]{:T(128)} %convert_element_type.34, () %tuple.115, (s32[8]{0:T(128)S(1)}, f32[8,2,2,128]{0,2,3,1:T(2,128)S(1)}, bf16[2,128,256]{2,1,0:T(8,128)(2,1)}) %tuple.116), branch_computations={%region_5.7_spmd, %region_6.8_spmd} | conditional | flops 100730880 | bytes 1730660 | solution.py:85
  83.0 9.3 %gather_fusion.1 = f32[1024,8,2,2]{1,3,2,0:T(2,128)} fusion(f32[8,2,2,128]{0,2,3,1:T(2,128)S(1)} %get-tuple-element.301, s32[1024]{0:T(1024)S(1)} %broadcast_clamp_fusion.1), kind=kCustom, calls=%fused_computation.1.clone | custom fusion | bytes 266240 | tf_op jit(solution)/shard_map/cond/branch_1_fun/jit(_take)/gather | solution.py:77
  92.4 3.5 %copy.546 = f32[128,8,8,2,2]{1,0,2,4,3:T(8,128)S(1)} copy(f32[128,8,8,2,2]{2,4,3,1,0:T(2,128)} %bitcast.187) | data formatting | bytes 262144 | tf_op jit(solution)/shard_map/cond/branch_1_fun/jit(_take)/gather | solution.py:77
  96.0 1.8 fusion.18
  98.0 5.6 %collective-permute-start.11 = (bf16[18,2,256]{2,1,0:T(2,128)(2,1)S(1)}, bf16[18,2,256]{2,1,0:T(2,128)(2,1)S(1)}, u32[]{:S(2)}, u32[]{:S(2)}) collective-permute-start(bf16[18,2,256]{2,1,0:T(2,128)(2,1)S(1)} %get-tuple-element.343), channel_id=1, source_target_pairs={{1,0},{2,1},{3,2},{4,3},{5,4},{6,5},{7,6},{8,7},{9,8},{10,9},{11,1... | collective-permute-start | bytes 55304 | tf_op jit(solution)/shard_map/ppermute | solution.py:21
  103.7 0.8 copy.523
  104.5 0.9 collective-permute-done.10
  105.4 0.8 slice_bitcast_fusion
  106.7 1.0 stack.59
  107.7 0.4 fusion.47
  108.1 0.9 copy.515
  109.0 0.9 copy.516
  110.0 0.9 copy.518
  111.0 1.6 copy.521
  112.6 1.6 copy.522
  114.2 0.8 copy.524
  115.0 0.7 copy.525
  115.7 2.1 stack.65
  117.8 1.4 convolution_add_fusion.1
  119.2 2.4 stack.71
  121.6 0.4 fusion.26
  122.4 1.8 convolution_bitcast_fusion
  124.8 0.5 fusion.53
  126.7 0.5 fusion.52
  128.4 5.7 %collective-permute-start.1 = (f32[18,2,256]{2,1,0:T(2,128)S(1)}, f32[18,2,256]{2,1,0:T(2,128)S(1)}, u32[]{:S(2)}, u32[]{:S(2)}) collective-permute-start(f32[18,2,256]{2,1,0:T(2,128)S(1)} %get-tuple-element.325), channel_id=1, source_target_pairs={{1,0},{2,1},{3,2},{4,3},{5,4},{6,5},{7,6},{8,7},{9,8},{10,9},{11,1... | collective-permute-start | bytes 110600 | tf_op jit(solution)/shard_map/ppermute | solution.py:21
  134.1 1.9 collective-permute-done
  136.1 2.1 collective-permute-start.2
  138.2 1.9 collective-permute-start.3
  140.1 39.7 %all_gather.6 = bf16[2,128,256]{2,1,0:T(8,128)(2,1)S(1)} all-gather(bf16[2,8,256]{2,1,0:T(8,128)(2,1)S(1)} %slice_select_fusion.1), channel_id=1, replica_groups=mesh['lat'=2,'lon'=16] {'lon'}, dimensions={1}, use_global_device_ids=true | all-gather | bytes 139264 | tf_op jit(solution)/shard_map/all_gather | solution.py:123
  179.9 16.5 %conditional.2 = (f32[2,8,256]{2,1,0:T(8,128)S(1)}) conditional(s32[]{:T(128)} %convert_element_type.34, () %tuple.113, (s32[8]{0:T(128)S(1)}, f32[8,2,2,128]{0,2,3,1:T(2,128)S(1)}, bf16[2,128,256]{2,1,0:T(8,128)(2,1)S(1)}, bf16[8,256,256]{2,1,0:T(8,128)(2,1)}) %tuple.114), branch_computations={%region_3.4_spmd, %region_4.6_spmd} | conditional | flops 369690624 | bytes 3975240 | solution.py:139
  180.0 9.3 %gather_fusion = f32[1024,8,2,2]{1,3,2,0:T(2,128)} fusion(f32[8,2,2,128]{0,2,3,1:T(2,128)S(1)} %get-tuple-element.297, s32[1024]{0:T(1024)S(1)} %broadcast_clamp_fusion), kind=kCustom, calls=%fused_computation.clone | custom fusion | bytes 266240 | tf_op jit(solution)/shard_map/cond/branch_1_fun/jit(_take)/gather | solution.py:128
  189.3 3.5 %copy.545 = f32[128,8,8,2,2]{1,0,2,4,3:T(8,128)S(1)} copy(f32[128,8,8,2,2]{2,4,3,1,0:T(2,128)} %bitcast.188) | data formatting | bytes 262144 | tf_op jit(solution)/shard_map/cond/branch_1_fun/jit(_take)/gather | solution.py:128
  192.9 1.7 fusion.3
  194.6 1.7 fusion.4
  196.5 1.3 collective-permute-start.5
  197.8 3.2 %collective-permute-done.4 = f32[1,8,256]{2,1,0:T(8,128)S(1)} collective-permute-done((f32[1,8,256]{2,1,0:T(8,128)S(1)}, f32[1,8,256]{2,1,0:T(8,128)S(1)}, u32[]{:S(2)}, u32[]{:S(2)}) %collective-permute-start.4) | collective-permute-done | bytes 8224 | tf_op jit(solution)/shard_map/ppermute | solution.py:31
  201.0 0.6 convert_element_type.35
  201.7 53.2 %all-reduce.3.cloned.1.call-done = f32[4,256,256]{2,1,0:T(8,128)} async-done(((f32[4,256,256]{2,1,0:T(8,128)}), f32[4,256,256]{2,1,0:T(8,128)}) %all-reduce.3.cloned.1.call-update) | async-done | bytes 1048592 | tf_op jit(solution)/shard_map/psum | solution.py:95
  254.9 2.3 copy.652
  (96 shorter events, 6.0 us)
Async XLA Ops:
  7.2 128.9 %reduce-scatter.2.cloned.1.call-start = ((), (), s32[]{:S(2)}) async-start(), calls=%async_computation.1 | async-start | bytes 3145728 | tf_op jit(solution)/shard_map/reduce_scatter | solution.py:89
  7.9 89.9 %collective-permute-start.7 = (bf16[1,8,256]{2,1,0:T(8,128)(2,1)S(1)}, bf16[1,8,256]{2,1,0:T(8,128)(2,1)S(1)}, u32[]{:S(2)}, u32[]{:S(2)}) collective-permute-start(bf16[1,8,256]{2,1,0:T(8,128)(2,1)S(1)} %get-tuple-element.348), channel_id=1, source_target_pairs={{0,16},{1,17},{2,18},{3,19},{4,20},{5,21},{6,22},{7,23},{8,24},{9,... | collective-permute-start | bytes 12296 | tf_op jit(solution)/shard_map/ppermute | solution.py:19
  10.3 87.6 %collective-permute-start.8 = (bf16[1,8,256]{2,1,0:T(8,128)(2,1)S(1)}, bf16[1,8,256]{2,1,0:T(8,128)(2,1)S(1)}, u32[]{:S(2)}, u32[]{:S(2)}) collective-permute-start(bf16[1,8,256]{2,1,0:T(8,128)(2,1)S(1)} %get-tuple-element.348), channel_id=1, source_target_pairs={{8,0},{9,1},{10,2},{11,3},{12,4},{13,5},{14,6},{15,7},{0,8},{1,9},... | collective-permute-start | bytes 12296 | tf_op jit(solution)/shard_map/ppermute | solution.py:31
  13.8 84.1 %collective-permute-start.6 = (bf16[1,8,256]{2,1,0:T(8,128)(2,1)S(1)}, bf16[1,8,256]{2,1,0:T(8,128)(2,1)S(1)}, u32[]{:S(2)}, u32[]{:S(2)}) collective-permute-start(bf16[1,8,256]{2,1,0:T(8,128)(2,1)S(1)} %get-tuple-element.347), channel_id=1, source_target_pairs={{8,0},{9,1},{10,2},{11,3},{12,4},{13,5},{14,6},{15,7},{0,8},{1,9},... | collective-permute-start | bytes 12296 | tf_op jit(solution)/shard_map/ppermute | solution.py:31
  13.8 84.1 %collective-permute-start.9 = (bf16[1,8,256]{2,1,0:T(8,128)(2,1)S(1)}, bf16[1,8,256]{2,1,0:T(8,128)(2,1)S(1)}, u32[]{:S(2)}, u32[]{:S(2)}) collective-permute-start(bf16[1,8,256]{2,1,0:T(8,128)(2,1)S(1)} %get-tuple-element.347), channel_id=1, source_target_pairs={{16,0},{17,1},{18,2},{19,3},{20,4},{21,5},{22,6},{23,7},{24,8},{25... | collective-permute-start | bytes 12296 | tf_op jit(solution)/shard_map/ppermute | solution.py:21
  20.4 6.2 %copy-start.5 = (s32[3]{0:T(128)S(1)}, s32[3]{0:T(128)}, u32[]{:S(2)}) copy-start(s32[3]{0:T(128)} %constant.695.clone.1) | copy-start | bytes 40
  21.2 59.3 %copy-start = (bf16[16,8,256]{2,1,0:T(8,128)(2,1)S(1)}, bf16[16,8,256]{2,1,0:T(8,128)(2,1)}, u32[]{:S(2)}) copy-start(bf16[16,8,256]{2,1,0:T(8,128)(2,1)} %param.58) | copy-start | bytes 196612
  92.4 3.6 %copy-start.2 = (bf16[2,128,256]{2,1,0:T(8,128)(2,1)S(1)}, bf16[2,128,256]{2,1,0:T(8,128)(2,1)}, u32[]{:S(2)}) copy-start(bf16[2,128,256]{2,1,0:T(8,128)(2,1)} %get-tuple-element.303) | copy-start | bytes 393220 | tf_op jit(solution)/shard_map/cond
  97.9 7.4 %collective-permute-start.10 = (bf16[18,2,256]{2,1,0:T(2,128)(2,1)S(1)}, bf16[18,2,256]{2,1,0:T(2,128)(2,1)S(1)}, u32[]{:S(2)}, u32[]{:S(2)}) collective-permute-start(bf16[18,2,256]{2,1,0:T(2,128)(2,1)S(1)} %get-tuple-element.344), channel_id=1, source_target_pairs={{0,1},{1,2},{2,3},{3,4},{4,5},{5,6},{6,7},{7,8},{8,9},{9,10},{10,1... | collective-permute-start | bytes 55304 | tf_op jit(solution)/shard_map/ppermute | solution.py:19
  98.0 7.3 %collective-permute-start.11 = (bf16[18,2,256]{2,1,0:T(2,128)(2,1)S(1)}, bf16[18,2,256]{2,1,0:T(2,128)(2,1)S(1)}, u32[]{:S(2)}, u32[]{:S(2)}) collective-permute-start(bf16[18,2,256]{2,1,0:T(2,128)(2,1)S(1)} %get-tuple-element.343), channel_id=1, source_target_pairs={{1,0},{2,1},{3,2},{4,3},{5,4},{6,5},{7,6},{8,7},{9,8},{10,9},{11,1... | collective-permute-start | bytes 55304 | tf_op jit(solution)/shard_map/ppermute | solution.py:21
  106.7 9.1 %copy-start.1 = (bf16[16,1,8,256]{3,1,2,0:T(2,128)(2,1)S(1)}, bf16[16,1,8,256]{3,1,2,0:T(2,128)(2,1)}, u32[]{:S(2)}) copy-start(bf16[16,1,8,256]{3,1,2,0:T(2,128)(2,1)} %copy.517) | copy-start | bytes 196612
  107.7 3.2 %copy-start.3 = (bf16[16,1,8,256]{3,2,0,1:T(8,128)(2,1)S(1)}, bf16[16,1,8,256]{3,2,0,1:T(8,128)(2,1)}, u32[]{:S(2)}) copy-start(bf16[16,1,8,256]{3,2,0,1:T(8,128)(2,1)} %get-tuple-element.329) | copy-start | bytes 196612
  121.6 0.8 copy-start.4
  124.3 130.6 %all-reduce.3.cloned.1.call-start = ((), (), s32[]{:S(2)}) async-start(), calls=%async_computation.2 | async-start | bytes 2097152 | tf_op jit(solution)/shard_map/psum | solution.py:95
  128.3 7.6 %collective-permute-start = (f32[18,2,256]{2,1,0:T(2,128)S(1)}, f32[18,2,256]{2,1,0:T(2,128)S(1)}, u32[]{:S(2)}, u32[]{:S(2)}) collective-permute-start(f32[18,2,256]{2,1,0:T(2,128)S(1)} %get-tuple-element.326), channel_id=1, source_target_pairs={{0,1},{1,2},{2,3},{3,4},{4,5},{5,6},{6,7},{7,8},{8,9},{9,10},{10,1... | collective-permute-start | bytes 110600 | tf_op jit(solution)/shard_map/ppermute | solution.py:19
  128.4 7.6 %collective-permute-start.1 = (f32[18,2,256]{2,1,0:T(2,128)S(1)}, f32[18,2,256]{2,1,0:T(2,128)S(1)}, u32[]{:S(2)}, u32[]{:S(2)}) collective-permute-start(f32[18,2,256]{2,1,0:T(2,128)S(1)} %get-tuple-element.325), channel_id=1, source_target_pairs={{1,0},{2,1},{3,2},{4,3},{5,4},{6,5},{7,6},{8,7},{9,8},{10,9},{11,1... | collective-permute-start | bytes 110600 | tf_op jit(solution)/shard_map/ppermute | solution.py:21
  136.1 61.7 %collective-permute-start.2 = (f32[1,8,256]{2,1,0:T(8,128)S(1)}, f32[1,8,256]{2,1,0:T(8,128)S(1)}, u32[]{:S(2)}, u32[]{:S(2)}) collective-permute-start(f32[1,8,256]{2,1,0:T(8,128)S(1)} %get-tuple-element.340), channel_id=1, source_target_pairs={{8,0},{9,1},{10,2},{11,3},{12,4},{13,5},{14,6},{15,7},{0,8},{1,9},... | collective-permute-start | bytes 24584 | tf_op jit(solution)/shard_map/ppermute | solution.py:31
  138.2 59.6 %collective-permute-start.3 = (f32[1,8,256]{2,1,0:T(8,128)S(1)}, f32[1,8,256]{2,1,0:T(8,128)S(1)}, u32[]{:S(2)}, u32[]{:S(2)}) collective-permute-start(f32[1,8,256]{2,1,0:T(8,128)S(1)} %get-tuple-element.339), channel_id=1, source_target_pairs={{0,16},{1,17},{2,18},{3,19},{4,20},{5,21},{6,22},{7,23},{8,24},{9,... | collective-permute-start | bytes 24584 | tf_op jit(solution)/shard_map/ppermute | solution.py:19
  196.4 4.6 %collective-permute-start.4 = (f32[1,8,256]{2,1,0:T(8,128)S(1)}, f32[1,8,256]{2,1,0:T(8,128)S(1)}, u32[]{:S(2)}, u32[]{:S(2)}) collective-permute-start(f32[1,8,256]{2,1,0:T(8,128)S(1)} %get-tuple-element.339), channel_id=1, source_target_pairs={{8,0},{9,1},{10,2},{11,3},{12,4},{13,5},{14,6},{15,7},{0,8},{1,9},... | collective-permute-start | bytes 24584 | tf_op jit(solution)/shard_map/ppermute | solution.py:31
  196.5 4.5 %collective-permute-start.5 = (f32[1,8,256]{2,1,0:T(8,128)S(1)}, f32[1,8,256]{2,1,0:T(8,128)S(1)}, u32[]{:S(2)}, u32[]{:S(2)}) collective-permute-start(f32[1,8,256]{2,1,0:T(8,128)S(1)} %get-tuple-element.340), channel_id=1, source_target_pairs={{16,0},{17,1},{18,2},{19,3},{20,4},{21,5},{22,6},{23,7},{24,8},{25... | collective-permute-start | bytes 24584 | tf_op jit(solution)/shard_map/ppermute | solution.py:21
Sparse Core Ops, SparseCore 0:
  124.4 10.9 reduce-scatter.1
  141.6 113.2 all-reduce.2
where the time goes:
time: 265 us; the launch traced here: 264 us
  blocking collectives  83.9 us (32%)
  waiting for transfers between devices  59.2 us (22%)
  local copies, waits for them, and re-layouts  58.9 us (22%)
  starting transfers between devices  24.2 us (9%)
  between operations  14.8 us (6%)
  matrix products  11.7 us (4%)
  other arithmetic  11.1 us (4%)
    psum x1, waiting for transfers between devices, on_device(): grad_weights = lax.psum(band_grad, 'lon')  53.2 us
    all_gather x1, blocking collectives, on_device(): block_rows = lax.all_gather(polar_in, 'lon', axis=1, tiled=True)  44.2 us
    all_gather x1, blocking collectives, on_device(): add_block_rows = lax.all_gather(polar_cot, 'lon', axis=1, tiled=True)  39.7 us
    gather x4, local copies, waits for them, and re-layouts, compute(): circulant = jnp.take(hemisphere, offset_idx, axis=3)  25.7 us
    another operation x19, local copies, waits for them, and re-layouts, on_device(): jnp.stack([widened[row_off:row_off + lat_rows, col_off:col_off + lon_cols...  15.9 us
    ppermute x4, starting transfers between devices, padded(): lax.ppermute(head, axis, [((i + 1) % count, i) for i in range(ends)])  13.8 us
    scatter-add x13, local copies, waits for them, and re-layouts, on_device(): grad_wide = grad_wide.at[row_off:row_off + lat_rows, col_off:col_off + lo...  7.81 us
    another operation x6, other arithmetic  6.64 us
  transfers between devices with their start and end apart: 14, of which 4 were waited for; matrix products, arithmetic and copies ran while one was open for 23% of the time, Pallas kernels for 0%

commit v1 on v0

--- a/solution.py
+++ b/solution.py
@@ -1,6 +1,11 @@
+import functools
+
 import jax
 import jax.numpy as jnp
+import numpy as np
 from jax import lax
+from jax.experimental import pallas as pl
+from jax.experimental.pallas import tpu as pltpu
 from jax.sharding import PartitionSpec as P
 
 RADIUS = 1
@@ -142,6 +147,287 @@
     return (interior.astype(jnp.bfloat16), grad_weights)
 
 
+COLS = 8
+SLOTS = 32
+MESH = pl.DeviceIdType.MESH
+
+
+def spread_matrices():
+    taps = 2 * REACH + 1
+    forward = np.zeros((2, 3, taps, 2, COLS, 4, SLOTS), np.float32)
+    backward = np.zeros((4, 3, taps, 2, COLS, 4, SLOTS), np.float32)
+    for inner in range(2):
+        for col in range(COLS):
+            for row in range(4):
+                for slot in range(SLOTS):
+                    a, b = row - inner, slot - COLS - col + REACH
+                    if 0 <= a < 3 and 0 <= b < taps:
+                        forward[inner, a, b, inner, col, row, slot] = 1
+                    a, b = inner - row + 2, col + REACH - (slot - COLS)
+                    if 0 <= a < 3 and 0 <= b < taps:
+                        backward[row, a, b, inner, col, row, slot] = 1
+    return forward.reshape(2 * 3 * taps, -1), backward.reshape(4 * 3 * taps, -1)
+
+
+def split(values):
+    high = values.astype(jnp.bfloat16)
+    return high, (values - high.astype(jnp.float32)).astype(jnp.bfloat16)
+
+
+def mul(a, b, dims=((1,), (0,))):
+    return lax.dot_general(a, b, (dims, ((), ())), preferred_element_type=jnp.float32)
+
+
+def fused(
+    n, f_ref, c_ref, w_ref, t1_ref, t2_ref, a_ref, b_ref, gf_ref, gw_ref,
+    fc, polar, sides, below, near, ext, sums, own, sib_out, sib_in, part, terms, mine, t2n,
+    acc, send_polar, recv_polar, send_misc, recv_misc, send_sib, recv_sib,
+    send_rs, recv_rs, send_ag, recv_ag,
+):
+    f32, bf16 = jnp.float32, jnp.bfloat16
+    lat, lon = lax.axis_index("lat"), lax.axis_index("lon")
+    points, channels = f_ref.shape
+    rows = points // COLS
+    pairs = rows // 2
+    kernels = w_ref.shape[0]
+    half_k = kernels // 2
+    chunk = half_k * channels // n
+    other = 1 - lat
+    north = lat == 0
+
+    def turn(t):
+        return lax.rem(lon + t, n)
+
+    barrier = pltpu.get_barrier_semaphore()
+    for t in range(1, n):
+        pl.semaphore_signal(barrier, inc=1, device_id=(lat, turn(t)), device_id_type=MESH)
+    for t in (0, 1, n - 1):
+        pl.semaphore_signal(barrier, inc=1, device_id=(other, turn(t)), device_id_type=MESH)
+    fc[0] = f_ref[...]
+    fc[1] = c_ref[...]
+    pl.semaphore_wait(barrier, n + 2)
+
+    def push(src, dst, send, recv, to):
+        copy = pltpu.make_async_remote_copy(
+            src_ref=src, dst_ref=dst, send_sem=send, recv_sem=recv, device_id=to, device_id_type=MESH
+        )
+        copy.start()
+        return copy
+
+    pole_at = pl.multiple_of(lat * (points - 16), 16)
+    edge_at = pl.multiple_of(other * (points - 16), 16)
+    edge = fc.at[:, pl.ds(edge_at, 16)]
+    first = [
+        push(fc, sides.at[0], send_misc.at[0], recv_misc.at[0], (lat, turn(1))),
+        push(fc, sides.at[1], send_misc.at[1], recv_misc.at[1], (lat, turn(n - 1))),
+        push(edge, below.at[1], send_misc.at[2], recv_misc.at[2], (other, lon)),
+        push(edge, below.at[0], send_misc.at[3], recv_misc.at[3], (other, turn(1))),
+        push(edge, below.at[2], send_misc.at[4], recv_misc.at[4], (other, turn(n - 1))),
+        push(t2_ref.at[pairs], near, send_misc.at[5], recv_misc.at[5], (other, lon)),
+    ]
+    for t in range(1, n):
+        first.append(
+            push(
+                fc.at[:, pl.ds(pole_at, 16)], polar.at[n - t],
+                send_polar.at[t], recv_polar.at[n - t], (lat, turn(t)),
+            )
+        )
+    polar[0] = fc[:, pl.ds(pole_at, 16)]
+    for copy in first:
+        copy.wait()
+
+    def block3(left, mid, right):
+        lead = mid.shape[:-2]
+        return jnp.concatenate([left, mid, right, jnp.zeros(lead + (COLS, channels), f32)], -2)
+
+    poles = []
+    for field in range(2):
+        gathered = polar[:, field].astype(f32).reshape(n, 2, COLS, channels)
+        pole_rows = [gathered[:, r].reshape(n * COLS, channels) for r in range(2)]
+        poles.append(jnp.concatenate(pole_rows, 0).astype(bf16))
+        inside = block3(
+            sides[0, field].astype(f32).reshape(rows, COLS, channels),
+            fc[field].astype(f32).reshape(rows, COLS, channels),
+            sides[1, field].astype(f32).reshape(rows, COLS, channels),
+        )
+        ext[field, pl.ds(SLOTS, rows * SLOTS)] = inside.reshape(rows * SLOTS, channels).astype(bf16)
+        turned = gathered[n // 2 - 1 : n // 2 + 2]
+        turned = jnp.where(north, turned[:, 0], turned[:, 1])
+        beside = below[:, field].astype(f32).reshape(3, 2, COLS, channels)
+        beside = jnp.where(north, beside[:, 0], beside[:, 1])
+        zeros = jnp.zeros((COLS, channels), f32)
+        top = jnp.where(north, turned, beside).reshape(3 * COLS, channels)
+        bottom = jnp.where(north, beside, turned).reshape(3 * COLS, channels)
+        ext[field, pl.ds(0, SLOTS)] = jnp.concatenate([top, zeros], 0).astype(bf16)
+        ext[field, pl.ds((rows + 1) * SLOTS, SLOTS)] = jnp.concatenate([bottom, zeros], 0).astype(bf16)
+
+    high, low = split(a_ref[...])
+    zonal = mul(high, poles[0]) + mul(low, poles[0])
+    for p in range(pairs):
+        taps = t1_ref[p].reshape(kernels * 16, 4 * SLOTS)
+        value = mul(taps, ext[0, pl.ds(2 * p * SLOTS, 4 * SLOTS)])
+        if p == 0:
+            value = value + jnp.where(north, zonal, 0.0)
+        if p == pairs - 1:
+            value = value + jnp.where(north, 0.0, zonal)
+        sums[:, pl.ds(16 * p, 16)] = value.astype(bf16).reshape(kernels, 16, channels)
+
+    cot = c_ref[...]
+    to_sib = []
+    for j in range(half_k):
+        at = pl.ds(j * channels, channels)
+        sib_out[at] = mul(sums[other * half_k + j], cot, ((0,), (0,))).astype(bf16)
+        to_sib.append(
+            push(sib_out.at[at], sib_in.at[at], send_sib.at[j], recv_sib.at[j], (other, lon))
+        )
+    for j in range(half_k):
+        own[pl.ds(j * channels, channels)] = mul(sums[lat * half_k + j], cot, ((0,), (0,)))
+    for j in range(half_k):
+        at = pl.ds(j * channels, channels)
+        to_sib[j].wait()
+        part[at] = (own[at] + sib_in[at].astype(f32)).astype(bf16)
+    scatter = []
+    for t in range(1, n):
+        at = pl.ds(pl.multiple_of(turn(t) * chunk, chunk), chunk)
+        scatter.append(
+            push(part.at[at], terms.at[t], send_rs.at[t], recv_rs.at[t], (lat, turn(t)))
+        )
+
+    edge_pair = (pairs - 1) * (1 - lat)
+    t2n[...] = near[...]
+    acc[...] = jnp.zeros_like(acc)
+    pole_acc = jnp.zeros((16, channels), f32)
+    near_acc = jnp.zeros((16, channels), f32)
+
+    def per_kernel(k, carry):
+        pole_acc, near_acc = carry
+        weight = w_ref[k]
+        grad = mul(ext[1], weight, ((1,), (1,))).astype(bf16)
+        for p in range(pairs):
+            window = grad[2 * p * SLOTS : (2 * p + 4) * SLOTS]
+            acc[pl.ds(16 * p, 16)] += mul(t2_ref[p, k], window)
+        last = grad[(2 * pairs - 2) * SLOTS : (2 * pairs + 2) * SLOTS]
+        near_acc += mul(t2n[k], jnp.where(north, last, grad[: 4 * SLOTS]))
+        pole_grad = mul(poles[1], weight, ((1,), (1,))).astype(bf16)
+        high, low = split(b_ref[k])
+        pole_acc += mul(high, pole_grad) + mul(low, pole_grad)
+        return pole_acc, near_acc
+
+    pole_acc, near_acc = lax.fori_loop(0, kernels, per_kernel, (pole_acc, near_acc))
+    acc[pl.ds(0, 16)] += jnp.where(north, pole_acc, near_acc)
+    acc[pl.ds(points - 16, 16)] += jnp.where(north, near_acc, pole_acc)
+    gf_ref[...] = acc[...].astype(bf16)
+
+    here = pl.ds(pl.multiple_of(lon * chunk, chunk), chunk)
+    total = part[here].astype(f32)
+    for t in range(1, n):
+        scatter[t - 1].wait()
+        total = total + terms[t].astype(f32)
+    mine[...] = total.astype(bf16)
+    gw_ref[here] = mine[...]
+    gather = []
+    for t in range(1, n):
+        gather.append(push(mine, gw_ref.at[here], send_ag.at[t], recv_ag.at[t], (lat, turn(t))))
+    for copy in gather:
+        copy.wait()
+
+
+def in_kernel(features, cotangent, weights, basis, polar_kernel, lon_reach):
+    lat_rows, lon_cols, channels = features.shape
+    kernels = weights.shape[0]
+    n = lax.axis_size("lon")
+    north = lax.axis_index("lat") == 0
+    pairs, points = lat_rows // 2, lat_rows * lon_cols
+    lon_total = lon_cols * n
+    offsets = jnp.abs(jnp.arange(2 * REACH + 1, dtype=jnp.int32) - REACH)
+    reach_mask = offsets[None, :] <= lon_reach[:, None]
+    masked = jnp.where(reach_mask[None, :, None, :], basis, 0)
+    spread, back = spread_matrices()
+    by_row = jnp.swapaxes(masked, 0, 1)
+    flat = by_row.reshape(pairs, 2, kernels, -1).swapaxes(1, 2).reshape(pairs, kernels, -1)
+    t1 = jnp.einsum("pkz,zn->pkn", flat, jnp.asarray(spread, jnp.bfloat16))
+    t1 = t1.reshape(pairs, kernels, 16, 4 * SLOTS)
+    zero_row = jnp.zeros_like(by_row[:1])
+    crossed_top = zero_row.at[0, :, 2].set(by_row[0, :, 0])
+    crossed_end = zero_row.at[0, :, 0].set(by_row[-1, :, 2])
+    longer = jnp.concatenate(
+        [jnp.where(north, crossed_top, 0), by_row, jnp.where(north, 0, crossed_end)], 0
+    )
+    quad = jnp.stack([longer[q : q + lat_rows - 1 : 2] for q in range(4)], 2)
+    gap = jnp.zeros_like(by_row[:3])
+    edge = jnp.where(
+        north, jnp.concatenate([by_row[-1:], gap], 0), jnp.concatenate([gap, by_row[:1]], 0)
+    )
+    quad = jnp.concatenate([quad, edge.swapaxes(0, 1)[None]], 0)
+    quad = quad.reshape(pairs + 1, kernels, -1)
+    t2 = jnp.einsum("pkz,zn->pkn", quad, jnp.asarray(back, jnp.bfloat16))
+    t2 = t2.reshape(pairs + 1, kernels, 16, 4 * SLOTS)
+    zonal = jnp.where(north, polar_kernel[:, 0], polar_kernel[:, 1])
+    twice = jnp.concatenate([zonal, zonal], 3)
+    a = jnp.stack(
+        [twice[..., lon_total - j : 2 * lon_total - j] for j in range(COLS)], 2
+    ).reshape(kernels * 16, 2 * lon_total)
+    twice = twice[..., ::-1]
+    b = jnp.stack(
+        [twice[..., lon_total - 1 - j : 2 * lon_total - 1 - j] for j in range(COLS)], 3
+    )
+    b = jnp.transpose(b, (0, 2, 3, 1, 4)).reshape(kernels, 16, 2 * lon_total)
+    half = kernels * channels // 2
+    bf16, f32 = jnp.bfloat16, jnp.float32
+    dma = pltpu.SemaphoreType.DMA
+    vmem = pl.BlockSpec(memory_space=pltpu.VMEM)
+    grad_features, grad_weights = pl.pallas_call(
+        functools.partial(fused, n),
+        out_shape=(
+            jax.ShapeDtypeStruct((points, channels), bf16),
+            jax.ShapeDtypeStruct((half, channels), bf16),
+        ),
+        in_specs=[vmem] * 7,
+        out_specs=(vmem, vmem),
+        scratch_shapes=[
+            pltpu.VMEM((2, points, channels), bf16),
+            pltpu.VMEM((n, 2, 16, channels), bf16),
+            pltpu.VMEM((2, 2, points, channels), bf16),
+            pltpu.VMEM((3, 2, 16, channels), bf16),
+            pltpu.VMEM((kernels, 16, 4 * SLOTS), bf16),
+            pltpu.VMEM((2, (lat_rows + 2) * SLOTS, channels), bf16),
+            pltpu.VMEM((kernels, points, channels), bf16),
+            pltpu.VMEM((half, channels), f32),
+            pltpu.VMEM((half, channels), bf16),
+            pltpu.VMEM((half, channels), bf16),
+            pltpu.VMEM((half, channels), bf16),
+            pltpu.VMEM((n, half // n, channels), bf16),
+            pltpu.VMEM((half // n, channels), bf16),
+            pltpu.VMEM((kernels, 16, 4 * SLOTS), bf16),
+            pltpu.VMEM((points, channels), f32),
+            dma((n,)), dma((n,)), dma((6,)), dma((6,)), dma((4,)), dma((4,)),
+            dma((n,)), dma((n,)), dma((n,)), dma((n,)),
+        ],
+        compiler_params=pltpu.CompilerParams(
+            collective_id=0, has_side_effects=True, vmem_limit_bytes=32 * 2**20
+        ),
+    )(
+        features.reshape(points, channels), cotangent.reshape(points, channels),
+        weights, t1, t2, a, b,
+    )
+    return (
+        grad_features.reshape(features.shape),
+        grad_weights.astype(f32).reshape(kernels // 2, channels, channels),
+    )
+
+
+def choose(features, cotangent, weights, basis, polar_kernel, lon_reach):
+    rows, cols, channels = features.shape
+    n = lax.axis_size("lon")
+    kernels = weights.shape[0]
+    fits = (
+        lax.axis_size("lat") == 2 and cols == COLS and n % 2 == 0 and n >= 4 and rows % 2 == 0
+        and rows >= 4 and kernels == 8 and (kernels // 2 * channels) % (16 * n) == 0
+    )
+    plan = in_kernel if fits else on_device
+    return plan(features, cotangent, weights, basis, polar_kernel, lon_reach)
+
+
 def solution(mesh):
     in_specs = (
         P("lat", "lon", None),
@@ -153,5 +439,5 @@
     )
     out_specs = (P("lat", "lon", None), P("lat", None, None))
     return jax.shard_map(
-        on_device, mesh=mesh, in_specs=in_specs, out_specs=out_specs, check_vma=False
-    )
+        choose, mesh=mesh, in_specs=in_specs, out_specs=out_specs, check_vma=False
+    )

time: 265 us -> 60.5 us (0.23)
  the two profiles are of different devices: /device:TPU:0 before, /device:TPU:28 now
where the time goes in v1:
time: 60.5 us; the launch traced here: 60.2 us
  Pallas kernels  44.2 us (73%)
  local copies, waits for them, and re-layouts  7.87 us (13%)
  other arithmetic  6.71 us (11%)
  between operations  0.96 us (2%)
    pallas_call x1, Pallas kernels, in_kernel(): pl.pallas_call(functools.partial(fused, n), out_shape=(jax.ShapeDtypeStru...  44.2 us
    unnamed x26, local copies, waits for them, and re-layouts  3.66 us
    another operation x2, other arithmetic  2.07 us
    slice x4, local copies, waits for them, and re-layouts, in_kernel(): quad = jnp.stack([longer[q:q + lat_rows - 1:2] for q in range(4)], 2)  1.46 us
    select_n x1, other arithmetic, in_kernel(): jnp.where(north, crossed_top, 0)  1.35 us

profile of v1, /device:TPU:28, one launch (start us, length us, event | category | flops | bytes accessed | tf_op | source)
XLA Modules:
  0.0 60.2 jit_solution(16166759624602111004)
XLA Ops:
  0.6 0.0 copy-start.8
  0.7 0.6 %copy-done.8 = s32[16]{0:T(128)S(1)} copy-done((s32[16]{0:T(128)S(1)}, s32[16]{0:T(128)}, u32[]{:S(2)}) %copy-start.8) | copy-done | bytes 88
  1.3 0.0 copy-start.7
  1.3 0.1 broadcast_compare_fusion
  1.4 0.0 copy-start.6
  1.4 0.6 fusion.31
  2.0 0.0 copy-done.7
  2.0 2.1 %and_reduce_fusion = pred[]{:T(512)} fusion(s32[4]{0:T(128)S(1)} %copy-done.7, s32[1]{0:T(128)} %constant.71.clone.1, s32[1]{0:T(128)} %get-tuple-element.43, s32[1]{0:T(128)} %get-tuple-element.42), kind=kLoop, calls=%fused_computation.83 | loop fusion | flops 27 | bytes 29 | tf_op jit(solution)/shard_map/reduce.2
  4.0 0.7 %fusion.29 = f32[8,2,2,128]{3,2,1,0:T(2,128)S(1)} fusion(f32[8,2,2,2,128]{4,3,2,1,0:T(2,128)} %param.16, pred[]{:T(512)S(6)} %eq.3), kind=kLoop, calls=%fused_computation.87 | loop fusion | flops 4096 | bytes 49153 | tf_op jit(solution)/shard_map/jit(_where)/select_n | solution.py:365
  4.8 0.0 copy-done.6
  4.8 0.4 slice.164
  5.2 0.4 slice.163
  5.6 1.3 %fusion.27 = (bf16[1,8,3,5]{0,1,3,2:T(8,128)(2,1)S(1)}, bf16[1,8,1,5]{0,1,3,2:T(8,128)(2,1)S(1)}) fusion(bf16[1,8,3,5]{0,1,3,2:T(8,128)(2,1)S(1)} %broadcast_in_dim.26, s32[]{:T(128)} %bitcast.7, bf16[16,8,3,5]{0,1,3,2:T(8,128)(2,1)S(1)} %select_bitcast_fusion.1, pred[]{:T(512)} %and_reduce_fusion, pred[]{:T(512)S(6)} %eq.3), kind=kLoop, calls=%fused_computation.81 | loop fusion | flops 80 | bytes 40966 | tf_op jit(solution)/shard_map/jit(_where)/select_n | solution.py:354
  6.9 0.1 pad_maximum_fusion.1
  7.0 0.4 slice.165
  7.4 0.4 slice.162
  7.8 0.2 copy.29
  8.0 0.1 copy.25
  8.1 0.2 copy.26
  8.3 0.1 reshape.182
  8.3 0.1 fusion.30
  8.4 0.1 select_bitcast_fusion
  8.5 0.3 copy.28
  8.8 0.0 copy-start.5
  8.8 0.1 concatenate.31
  8.9 0.7 %copy-done.5 = f32[8,2,2,2,128]{4,3,2,1,0:T(2,128)S(1)} copy-done((f32[8,2,2,2,128]{4,3,2,1,0:T(2,128)S(1)}, f32[8,2,2,2,128]{4,3,2,1,0:T(2,128)}, u32[]{:S(2)}) %copy-start.5) | copy-done | bytes 32792
  9.6 0.1 constant_dynamic-update-slice_fusion.6
  9.7 0.1 constant_dynamic-update-slice_fusion.5
  9.9 0.1 constant_dynamic-update-slice_fusion.4
  10.0 0.1 constant_dynamic-update-slice_fusion.3
  10.1 0.1 constant_dynamic-update-slice_fusion.2
  10.2 0.1 constant_dynamic-update-slice_fusion.1
  10.4 0.1 constant_dynamic-update-slice_fusion
  10.5 0.1 copy.30
  10.6 0.3 pad_maximum_fusion.2
  10.9 0.1 slice.192
  11.0 0.1 slice.178
  11.1 0.1 slice.180
  11.3 0.1 slice.182
  11.4 0.1 slice.184
  11.5 0.1 slice.186
  11.6 0.1 slice.188
  11.7 0.1 slice.190
  11.9 0.0 copy-start.4
  12.0 0.0 copy-start.3
  12.0 0.1 copy.39
  12.1 0.8 %copy-done.4 = bf16[16,128,30,1]{1,2,0,3:T(8,128)(2,1)S(1)} copy-done((bf16[16,128,30,1]{1,2,0,3:T(8,128)(2,1)S(1)}, bf16[16,128,30,1]{1,2,0,3:T(8,128)(2,1)}, u32[]{:S(2)}) %copy-start.4) | copy-done | bytes 122904
  12.8 0.0 copy-start
  12.8 0.2 fusion.24
  13.1 0.0 copy-done.3
  13.1 0.2 fusion
  13.3 0.0 copy-start.1
  13.3 0.0 copy-start.2
  13.4 0.7 %copy-done = bf16[8,256,256]{2,1,0:T(8,128)(2,1)S(1)} copy-done((bf16[8,256,256]{2,1,0:T(8,128)(2,1)S(1)}, bf16[8,256,256]{2,1,0:T(8,128)(2,1)}, u32[]{:S(2)}) %copy-start) | copy-done | bytes 1048600
  14.1 0.2 copy-done.1
  14.2 0.0 copy-done.2
  14.3 44.2 %shard_map.95 = (bf16[128,256]{1,0:T(8,128)(2,1)S(1)}, bf16[1024,256]{1,0:T(8,128)(2,1)S(1)}) custom-call(bf16[128,256]{1,0:T(8,128)(2,1)S(1)} %bitcast.86, bf16[128,256]{1,0:T(8,128)(2,1)S(1)} %bitcast.87, bf16[8,256,256]{2,1,0:T(8,128)(2,1)S(1)} %copy-done, bf16[8,8,16,128]{3,2,1,0:T(8,128)(2,1)S(1)} %copy.32.t1_ref, ...), custom_call_target="tpu_custom_call" | custom-call | tf_op jit(solution)/shard_map/pallas_call | solution.py:379
  58.5 1.1 %convert.1 = f32[4,256,256]{2,1,0:T(8,128)} convert(bf16[4,256,256]{2,1,0:T(8,128)(2,1)S(1)} %bitcast.83) | non-fusion elementwise | flops 262144 | bytes 1572864 | tf_op jit(solution)/shard_map/reshape | solution.py:415
  59.5 0.6 %copy.56 = bf16[16,8,256]{2,1,0:T(8,128)(2,1)} copy(bf16[16,8,256]{2,1,0:T(8,128)(2,1)S(1)} %bitcast.88) | data formatting | bytes 131072
  (17 shorter events, 0.2 us)
Async XLA Ops:
  0.6 0.7 %copy-start.8 = (s32[16]{0:T(128)S(1)}, s32[16]{0:T(128)}, u32[]{:S(2)}) copy-start(s32[16]{0:T(128)} %param.17) | copy-start | bytes 196
  1.3 0.7 %copy-start.7 = (s32[4]{0:T(128)S(1)}, s32[4]{0:T(128)}, u32[]{:S(2)}) copy-start(s32[4]{0:T(128)} %constant.72.clone.1) | copy-start | bytes 52
  1.4 3.4 %copy-start.6 = (bf16[8,16,3,5]{1,0,3,2:T(8,128)(2,1)S(1)}, bf16[8,16,3,5]{1,0,3,2:T(8,128)(2,1)}, u32[]{:S(2)}) copy-start(bf16[8,16,3,5]{1,0,3,2:T(8,128)(2,1)} %param.15) | copy-start | bytes 11524
  8.8 0.8 %copy-start.5 = (f32[8,2,2,2,128]{4,3,2,1,0:T(2,128)S(1)}, f32[8,2,2,2,128]{4,3,2,1,0:T(2,128)}, u32[]{:S(2)}) copy-start(f32[8,2,2,2,128]{4,3,2,1,0:T(2,128)} %param.16) | copy-start | bytes 98308
  11.9 0.9 %copy-start.4 = (bf16[16,128,30,1]{1,2,0,3:T(8,128)(2,1)S(1)}, bf16[16,128,30,1]{1,2,0,3:T(8,128)(2,1)}, u32[]{:S(2)}) copy-start(bf16[16,128,30,1]{1,2,0,3:T(8,128)(2,1)} %constant.88) | copy-start | bytes 368644
  12.0 1.1 %copy-start.3 = (bf16[16,128,60,1]{1,2,0,3:T(8,128)(2,1)S(1)}, bf16[16,128,60,1]{1,2,0,3:T(8,128)(2,1)}, u32[]{:S(2)}) copy-start(bf16[16,128,60,1]{1,2,0,3:T(8,128)(2,1)} %constant.89) | copy-start | bytes 737284
  12.8 1.2 %copy-start = (bf16[8,256,256]{2,1,0:T(8,128)(2,1)S(1)}, bf16[8,256,256]{2,1,0:T(8,128)(2,1)}, u32[]{:S(2)}) copy-start(bf16[8,256,256]{2,1,0:T(8,128)(2,1)} %w_ref.1) | copy-start | bytes 3145732
  13.3 0.9 %copy-start.1 = (bf16[16,8,256]{2,1,0:T(8,128)(2,1)S(1)}, bf16[16,8,256]{2,1,0:T(8,128)(2,1)}, u32[]{:S(2)}) copy-start(bf16[16,8,256]{2,1,0:T(8,128)(2,1)} %param.12) | copy-start | bytes 196612
  13.3 0.9 %copy-start.2 = (bf16[16,8,256]{2,1,0:T(8,128)(2,1)S(1)}, bf16[16,8,256]{2,1,0:T(8,128)(2,1)}, u32[]{:S(2)}) copy-start(bf16[16,8,256]{2,1,0:T(8,128)(2,1)} %param.13) | copy-start | bytes 196612

commit v2 on v1

--- a/solution.py
+++ b/solution.py
@@ -154,19 +154,19 @@
 
 def spread_matrices():
     taps = 2 * REACH + 1
-    forward = np.zeros((2, 3, taps, 2, COLS, 4, SLOTS), np.float32)
-    backward = np.zeros((4, 3, taps, 2, COLS, 4, SLOTS), np.float32)
+    forward = np.zeros((16, 2, COLS, 4, SLOTS), np.float32)
+    backward = np.zeros((16, 2, COLS, 4, SLOTS), np.float32)
     for inner in range(2):
         for col in range(COLS):
             for row in range(4):
                 for slot in range(SLOTS):
                     a, b = row - inner, slot - COLS - col + REACH
                     if 0 <= a < 3 and 0 <= b < taps:
-                        forward[inner, a, b, inner, col, row, slot] = 1
+                        forward[a * taps + b, inner, col, row, slot] = 1
                     a, b = inner - row + 2, col + REACH - (slot - COLS)
                     if 0 <= a < 3 and 0 <= b < taps:
-                        backward[row, a, b, inner, col, row, slot] = 1
-    return forward.reshape(2 * 3 * taps, -1), backward.reshape(4 * 3 * taps, -1)
+                        backward[a * taps + b, inner, col, row, slot] = 1
+    return np.concatenate([forward.reshape(16, -1), backward.reshape(16, -1)], 1)
 
 
 def split(values):
@@ -179,9 +179,10 @@
 
 
 def fused(
-    n, f_ref, c_ref, w_ref, t1_ref, t2_ref, a_ref, b_ref, gf_ref, gw_ref,
-    fc, polar, sides, below, near, ext, sums, own, sib_out, sib_in, part, terms, mine, t2n,
-    acc, send_polar, recv_polar, send_misc, recv_misc, send_sib, recv_sib,
+    n, f_ref, c_ref, w_ref, m_ref, h_ref, d_ref, gf_ref, gw_ref,
+    fc, polar, packs, sides, below, rims, near, taps_f, taps_b, rev, circ, ext, sums, own,
+    sib_out, sib_in, part, terms, mine, acc,
+    send_polar, recv_polar, send_misc, recv_misc, send_sib, recv_sib,
     send_rs, recv_rs, send_ag, recv_ag,
 ):
     f32, bf16 = jnp.float32, jnp.bfloat16
@@ -192,6 +193,8 @@
     kernels = w_ref.shape[0]
     half_k = kernels // 2
     chunk = half_k * channels // n
+    window = 4 * SLOTS
+    lanes = 16 * window
     other = 1 - lat
     north = lat == 0
 
@@ -203,8 +206,25 @@
         pl.semaphore_signal(barrier, inc=1, device_id=(lat, turn(t)), device_id_type=MESH)
     for t in (0, 1, n - 1):
         pl.semaphore_signal(barrier, inc=1, device_id=(other, turn(t)), device_id_type=MESH)
+
     fc[0] = f_ref[...]
     fc[1] = c_ref[...]
+    place = lax.broadcasted_iota(jnp.int32, (COLS, channels), 0) // REACH
+    group = COLS // REACH
+    for field in range(2):
+        cells = fc[field].astype(f32)
+        for side in range(2):
+            packed = []
+            for g in range(rows // group):
+                block = jnp.zeros((COLS, channels), f32)
+                for u in range(group):
+                    row = cells[COLS * (group * g + u) : COLS * (group * g + u + 1)]
+                    shift = REACH * u + (REACH if side == 0 else 0)
+                    block = jnp.where(place == u, pltpu.roll(row, shift % COLS, 0), block)
+                packed.append(block)
+            packs[side, field] = jnp.concatenate(packed, 0).astype(bf16)
+    by_row = [m_ref[pl.ds(i, kernels, stride=rows), :] for i in range(rows)]
+    rims[...] = jnp.where(north, by_row[-1], by_row[0])
     pl.semaphore_wait(barrier, n + 2)
 
     def push(src, dst, send, recv, to):
@@ -216,72 +236,103 @@
 
     pole_at = pl.multiple_of(lat * (points - 16), 16)
     edge_at = pl.multiple_of(other * (points - 16), 16)
-    edge = fc.at[:, pl.ds(edge_at, 16)]
-    first = [
-        push(fc, sides.at[0], send_misc.at[0], recv_misc.at[0], (lat, turn(1))),
-        push(fc, sides.at[1], send_misc.at[1], recv_misc.at[1], (lat, turn(n - 1))),
-        push(edge, below.at[1], send_misc.at[2], recv_misc.at[2], (other, lon)),
-        push(edge, below.at[0], send_misc.at[3], recv_misc.at[3], (other, turn(1))),
-        push(edge, below.at[2], send_misc.at[4], recv_misc.at[4], (other, turn(n - 1))),
-        push(t2_ref.at[pairs], near, send_misc.at[5], recv_misc.at[5], (other, lon)),
+    arriving = []
+    for field in range(2):
+        edge = fc.at[field, pl.ds(edge_at, 16)]
+        pole = fc.at[field, pl.ds(pole_at, 16)]
+        copies = []
+        for t in sorted(range(1, n), key=lambda t: -min(t, n - t)):
+            copies.append(
+                push(
+                    pole, polar.at[field, n - t],
+                    send_polar.at[field, t], recv_polar.at[field, n - t], (lat, turn(t)),
+                )
+            )
+        routes = (
+            (packs.at[0, field], sides.at[0, field], (lat, turn(1))),
+            (packs.at[1, field], sides.at[1, field], (lat, turn(n - 1))),
+            (edge, below.at[field, 0], (other, turn(1))),
+            (edge, below.at[field, 2], (other, turn(n - 1))),
+            (edge, below.at[field, 1], (other, lon)),
+        )
+        for r, (src, dst, to) in enumerate(routes):
+            copies.append(push(src, dst, send_misc.at[field, r], recv_misc.at[field, r], to))
+        arriving.append(copies)
+        polar[field, 0] = fc[field, pl.ds(pole_at, 16)]
+    arriving[1].append(push(rims, near, send_misc.at[0, 5], recv_misc.at[0, 5], (other, lon)))
+
+    mat = jnp.concatenate(by_row, 0)
+    taps_f[...] = mul(mat[:, :16].astype(bf16), d_ref[:, :lanes]).astype(bf16).astype(f32)
+    zonal = [
+        [h_ref[pl.ds(lat * 4 + a * 2 + r, kernels, stride=8), :] for r in range(2)] for a in range(2)
     ]
-    for t in range(1, n):
-        first.append(
-            push(
-                fc.at[:, pl.ds(pole_at, 16)], polar.at[n - t],
-                send_polar.at[t], recv_polar.at[n - t], (lat, turn(t)),
-            )
-        )
-    polar[0] = fc[:, pl.ds(pole_at, 16)]
-    for copy in first:
-        copy.wait()
-
-    def block3(left, mid, right):
-        lead = mid.shape[:-2]
-        return jnp.concatenate([left, mid, right, jnp.zeros(lead + (COLS, channels), f32)], -2)
-
-    poles = []
-    for field in range(2):
-        gathered = polar[:, field].astype(f32).reshape(n, 2, COLS, channels)
+    rolled = [
+        jnp.concatenate([pltpu.roll(z, j, 1) if j else z for z in zonal[a]], 1)
+        for a in range(2)
+        for j in range(COLS)
+    ]
+    high, low = split(jnp.concatenate(rolled, 0))
+
+    def extend(field):
+        gathered = polar[field].astype(f32).reshape(n, 2, COLS, channels)
         pole_rows = [gathered[:, r].reshape(n * COLS, channels) for r in range(2)]
-        poles.append(jnp.concatenate(pole_rows, 0).astype(bf16))
-        inside = block3(
-            sides[0, field].astype(f32).reshape(rows, COLS, channels),
-            fc[field].astype(f32).reshape(rows, COLS, channels),
-            sides[1, field].astype(f32).reshape(rows, COLS, channels),
-        )
-        ext[field, pl.ds(SLOTS, rows * SLOTS)] = inside.reshape(rows * SLOTS, channels).astype(bf16)
+        zeros = jnp.zeros((COLS, channels), f32)
+        left, right = sides[0, field].astype(f32), sides[1, field].astype(f32)
+        cells = fc[field].astype(f32)
+        for i in range(rows):
+            g, u = i // group, i % group
+            ends = [side[COLS * g : COLS * (g + 1)] for side in (left, right)]
+            line = [
+                pltpu.roll(ends[0], (COLS - REACH - REACH * u) % COLS, 0),
+                cells[COLS * i : COLS * (i + 1)],
+                pltpu.roll(ends[1], (COLS - REACH * u) % COLS, 0),
+                zeros,
+            ]
+            ext[field, pl.ds((i + 1) * SLOTS, SLOTS)] = jnp.concatenate(line, 0).astype(bf16)
         turned = gathered[n // 2 - 1 : n // 2 + 2]
         turned = jnp.where(north, turned[:, 0], turned[:, 1])
-        beside = below[:, field].astype(f32).reshape(3, 2, COLS, channels)
+        beside = below[field].astype(f32).reshape(3, 2, COLS, channels)
         beside = jnp.where(north, beside[:, 0], beside[:, 1])
-        zeros = jnp.zeros((COLS, channels), f32)
         top = jnp.where(north, turned, beside).reshape(3 * COLS, channels)
         bottom = jnp.where(north, beside, turned).reshape(3 * COLS, channels)
         ext[field, pl.ds(0, SLOTS)] = jnp.concatenate([top, zeros], 0).astype(bf16)
         ext[field, pl.ds((rows + 1) * SLOTS, SLOTS)] = jnp.concatenate([bottom, zeros], 0).astype(bf16)
-
-    high, low = split(a_ref[...])
-    zonal = mul(high, poles[0]) + mul(low, poles[0])
+        return jnp.concatenate(pole_rows, 0).astype(bf16)
+
+    for copy in arriving[0]:
+        copy.wait()
+    poles = extend(0)
+    polar_part = mul(high, poles) + mul(low, poles)
     for p in range(pairs):
-        taps = t1_ref[p].reshape(kernels * 16, 4 * SLOTS)
-        value = mul(taps, ext[0, pl.ds(2 * p * SLOTS, 4 * SLOTS)])
+        taps = [
+            taps_f[kernels * (2 * p + x // COLS) : kernels * (2 * p + x // COLS + 1),
+                   x * window : (x + 1) * window]
+            for x in range(16)
+        ]
+        taps = jnp.concatenate(taps, 0).astype(bf16)
+        value = mul(taps, ext[0, pl.ds(2 * p * SLOTS, window)])
         if p == 0:
-            value = value + jnp.where(north, zonal, 0.0)
+            value = value + jnp.where(north, polar_part, 0.0)
         if p == pairs - 1:
-            value = value + jnp.where(north, 0.0, zonal)
-        sums[:, pl.ds(16 * p, 16)] = value.astype(bf16).reshape(kernels, 16, channels)
+            value = value + jnp.where(north, 0.0, polar_part)
+        for h in range(channels // 128):
+            sums[h, pl.ds(16 * kernels * p, 16 * kernels)] = value[:, 128 * h : 128 * (h + 1)]
 
     cot = c_ref[...]
+
+    def gradient(k):
+        cells = [sums[h, pl.ds(k, points, stride=kernels), :] for h in range(channels // 128)]
+        return mul(jnp.concatenate(cells, 1).astype(bf16), cot, ((0,), (0,)))
+
     to_sib = []
     for j in range(half_k):
         at = pl.ds(j * channels, channels)
-        sib_out[at] = mul(sums[other * half_k + j], cot, ((0,), (0,))).astype(bf16)
+        sib_out[at] = gradient(other * half_k + j).astype(bf16)
         to_sib.append(
             push(sib_out.at[at], sib_in.at[at], send_sib.at[j], recv_sib.at[j], (other, lon))
         )
     for j in range(half_k):
-        own[pl.ds(j * channels, channels)] = mul(sums[lat * half_k + j], cot, ((0,), (0,)))
+        own[pl.ds(j * channels, channels)] = gradient(lat * half_k + j)
     for j in range(half_k):
         at = pl.ds(j * channels, channels)
         to_sib[j].wait()
@@ -293,29 +344,62 @@
             push(part.at[at], terms.at[t], send_rs.at[t], recv_rs.at[t], (lat, turn(t)))
         )
 
-    edge_pair = (pairs - 1) * (1 - lat)
-    t2n[...] = near[...]
+    for copy in arriving[1]:
+        copy.wait()
+    poles = extend(1)
+    taps_each = 3 * (2 * REACH + 1)
+    step = 2 * (2 * REACH + 1)
+    lane = lax.broadcasted_iota(jnp.int32, (kernels, 128), 1)
+    first_taps = lane < taps_each - step
+    up = jnp.where(first_taps, by_row[0], 0.0)
+    up = pltpu.roll(up, step, 1)
+    down = pltpu.roll(by_row[-1], 128 - step, 1)
+    down = jnp.where(first_taps, down, 0.0)
+    beside = near[...]
+    mat = jnp.concatenate(
+        [jnp.where(north, up, beside)] + by_row + [jnp.where(north, beside, down)], 0
+    )
+    spread = mul(mat[:, :16].astype(bf16), d_ref[:, lanes:])
+    part_of = lax.broadcasted_iota(jnp.int32, (kernels, window), 1) // SLOTS
+    for p in range(pairs):
+        for x in range(16):
+            tile = jnp.zeros((kernels, window), f32)
+            for q in range(4):
+                i = kernels * (2 * p + q)
+                tile = jnp.where(
+                    part_of == q, spread[i : i + kernels, x * window : (x + 1) * window], tile
+                )
+            taps_b[pl.ds((16 * p + x) * kernels, kernels)] = tile
+    flip = lax.broadcasted_iota(jnp.int32, (128, 128), 0) + lax.broadcasted_iota(
+        jnp.int32, (128, 128), 1
+    )
+    flip = jnp.where(flip == 127, 1.0, 0.0).astype(bf16)
+    high, low = split(h_ref[...])
+    rev[...] = mul(high, flip) + mul(low, flip)
+    for r in range(2):
+        turned = [
+            rev[pl.ds(lat * 4 + a * 2 + r, kernels, stride=8), :] for a in range(2)
+        ]
+        for j in range(COLS):
+            for a in range(2):
+                circ[a, pl.ds((r * COLS + j) * kernels, kernels)] = pltpu.roll(turned[a], j + 1, 1)
     acc[...] = jnp.zeros_like(acc)
-    pole_acc = jnp.zeros((16, channels), f32)
-    near_acc = jnp.zeros((16, channels), f32)
-
-    def per_kernel(k, carry):
-        pole_acc, near_acc = carry
+
+    def per_kernel(k, pole_acc):
         weight = w_ref[k]
         grad = mul(ext[1], weight, ((1,), (1,))).astype(bf16)
         for p in range(pairs):
-            window = grad[2 * p * SLOTS : (2 * p + 4) * SLOTS]
-            acc[pl.ds(16 * p, 16)] += mul(t2_ref[p, k], window)
-        last = grad[(2 * pairs - 2) * SLOTS : (2 * pairs + 2) * SLOTS]
-        near_acc += mul(t2n[k], jnp.where(north, last, grad[: 4 * SLOTS]))
-        pole_grad = mul(poles[1], weight, ((1,), (1,))).astype(bf16)
-        high, low = split(b_ref[k])
-        pole_acc += mul(high, pole_grad) + mul(low, pole_grad)
-        return pole_acc, near_acc
-
-    pole_acc, near_acc = lax.fori_loop(0, kernels, per_kernel, (pole_acc, near_acc))
-    acc[pl.ds(0, 16)] += jnp.where(north, pole_acc, near_acc)
-    acc[pl.ds(points - 16, 16)] += jnp.where(north, near_acc, pole_acc)
+            taps = taps_b[pl.ds(16 * kernels * p + k, 16, stride=kernels), :].astype(bf16)
+            acc[pl.ds(16 * p, 16)] += mul(taps, grad[2 * p * SLOTS : 2 * p * SLOTS + window])
+        pole_grad = mul(poles, weight, ((1,), (1,))).astype(bf16)
+        high, low = split(
+            jnp.concatenate([circ[a, pl.ds(k, 16, stride=kernels), :] for a in range(2)], 1)
+        )
+        return pole_acc + mul(high, pole_grad) + mul(low, pole_grad)
+
+    pole_acc = lax.fori_loop(0, kernels, per_kernel, jnp.zeros((16, channels), f32))
+    acc[pl.ds(0, 16)] += jnp.where(north, pole_acc, 0.0)
+    acc[pl.ds(points - 16, 16)] += jnp.where(north, 0.0, pole_acc)
     gf_ref[...] = acc[...].astype(bf16)
 
     here = pl.ds(pl.multiple_of(lon * chunk, chunk), chunk)
@@ -336,44 +420,17 @@
     lat_rows, lon_cols, channels = features.shape
     kernels = weights.shape[0]
     n = lax.axis_size("lon")
-    north = lax.axis_index("lat") == 0
     pairs, points = lat_rows // 2, lat_rows * lon_cols
-    lon_total = lon_cols * n
+    taps = 3 * (2 * REACH + 1)
+    bf16, f32 = jnp.bfloat16, jnp.float32
     offsets = jnp.abs(jnp.arange(2 * REACH + 1, dtype=jnp.int32) - REACH)
     reach_mask = offsets[None, :] <= lon_reach[:, None]
     masked = jnp.where(reach_mask[None, :, None, :], basis, 0)
-    spread, back = spread_matrices()
-    by_row = jnp.swapaxes(masked, 0, 1)
-    flat = by_row.reshape(pairs, 2, kernels, -1).swapaxes(1, 2).reshape(pairs, kernels, -1)
-    t1 = jnp.einsum("pkz,zn->pkn", flat, jnp.asarray(spread, jnp.bfloat16))
-    t1 = t1.reshape(pairs, kernels, 16, 4 * SLOTS)
-    zero_row = jnp.zeros_like(by_row[:1])
-    crossed_top = zero_row.at[0, :, 2].set(by_row[0, :, 0])
-    crossed_end = zero_row.at[0, :, 0].set(by_row[-1, :, 2])
-    longer = jnp.concatenate(
-        [jnp.where(north, crossed_top, 0), by_row, jnp.where(north, 0, crossed_end)], 0
-    )
-    quad = jnp.stack([longer[q : q + lat_rows - 1 : 2] for q in range(4)], 2)
-    gap = jnp.zeros_like(by_row[:3])
-    edge = jnp.where(
-        north, jnp.concatenate([by_row[-1:], gap], 0), jnp.concatenate([gap, by_row[:1]], 0)
-    )
-    quad = jnp.concatenate([quad, edge.swapaxes(0, 1)[None]], 0)
-    quad = quad.reshape(pairs + 1, kernels, -1)
-    t2 = jnp.einsum("pkz,zn->pkn", quad, jnp.asarray(back, jnp.bfloat16))
-    t2 = t2.reshape(pairs + 1, kernels, 16, 4 * SLOTS)
-    zonal = jnp.where(north, polar_kernel[:, 0], polar_kernel[:, 1])
-    twice = jnp.concatenate([zonal, zonal], 3)
-    a = jnp.stack(
-        [twice[..., lon_total - j : 2 * lon_total - j] for j in range(COLS)], 2
-    ).reshape(kernels * 16, 2 * lon_total)
-    twice = twice[..., ::-1]
-    b = jnp.stack(
-        [twice[..., lon_total - 1 - j : 2 * lon_total - 1 - j] for j in range(COLS)], 3
-    )
-    b = jnp.transpose(b, (0, 2, 3, 1, 4)).reshape(kernels, 16, 2 * lon_total)
+    masked = masked.reshape(kernels * lat_rows, taps).astype(f32)
+    masked = jnp.pad(masked, ((0, 0), (0, 128 - taps)))
+    spread = jnp.asarray(spread_matrices(), bf16)
     half = kernels * channels // 2
-    bf16, f32 = jnp.bfloat16, jnp.float32
+    window, pack = 4 * SLOTS, lat_rows * REACH
     dma = pltpu.SemaphoreType.DMA
     vmem = pl.BlockSpec(memory_space=pltpu.VMEM)
     grad_features, grad_weights = pl.pallas_call(
@@ -382,33 +439,38 @@
             jax.ShapeDtypeStruct((points, channels), bf16),
             jax.ShapeDtypeStruct((half, channels), bf16),
         ),
-        in_specs=[vmem] * 7,
+        in_specs=[vmem] * 6,
         out_specs=(vmem, vmem),
         scratch_shapes=[
             pltpu.VMEM((2, points, channels), bf16),
-            pltpu.VMEM((n, 2, 16, channels), bf16),
-            pltpu.VMEM((2, 2, points, channels), bf16),
-            pltpu.VMEM((3, 2, 16, channels), bf16),
-            pltpu.VMEM((kernels, 16, 4 * SLOTS), bf16),
+            pltpu.VMEM((2, n, 16, channels), bf16),
+            pltpu.VMEM((2, 2, pack, channels), bf16),
+            pltpu.VMEM((2, 2, pack, channels), bf16),
+            pltpu.VMEM((2, 3, 16, channels), bf16),
+            pltpu.VMEM((kernels, 128), f32),
+            pltpu.VMEM((kernels, 128), f32),
+            pltpu.VMEM((lat_rows * kernels, 16 * window), f32),
+            pltpu.VMEM((pairs * 16 * kernels, window), f32),
+            pltpu.VMEM((kernels * 8, 128), f32),
+            pltpu.VMEM((2, 16 * kernels, lon_cols * n), f32),
             pltpu.VMEM((2, (lat_rows + 2) * SLOTS, channels), bf16),
-            pltpu.VMEM((kernels, points, channels), bf16),
+            pltpu.VMEM((channels // 128, points * kernels, 128), f32),
             pltpu.VMEM((half, channels), f32),
             pltpu.VMEM((half, channels), bf16),
             pltpu.VMEM((half, channels), bf16),
             pltpu.VMEM((half, channels), bf16),
             pltpu.VMEM((n, half // n, channels), bf16),
             pltpu.VMEM((half // n, channels), bf16),
-            pltpu.VMEM((kernels, 16, 4 * SLOTS), bf16),
             pltpu.VMEM((points, channels), f32),
-            dma((n,)), dma((n,)), dma((6,)), dma((6,)), dma((4,)), dma((4,)),
+            dma((2, n)), dma((2, n)), dma((2, 6)), dma((2, 6)), dma((4,)), dma((4,)),
             dma((n,)), dma((n,)), dma((n,)), dma((n,)),
         ],
         compiler_params=pltpu.CompilerParams(
-            collective_id=0, has_side_effects=True, vmem_limit_bytes=32 * 2**20
+            collective_id=0, has_side_effects=True, vmem_limit_bytes=40 * 2**20
         ),
     )(
         features.reshape(points, channels), cotangent.reshape(points, channels),
-        weights, t1, t2, a, b,
+        weights, masked, polar_kernel.reshape(kernels * 8, lon_cols * n), spread,
     )
     return (
         grad_features.reshape(features.shape),
@@ -421,8 +483,8 @@
     n = lax.axis_size("lon")
     kernels = weights.shape[0]
     fits = (
-        lax.axis_size("lat") == 2 and cols == COLS and n % 2 == 0 and n >= 4 and rows % 2 == 0
-        and rows >= 4 and kernels == 8 and (kernels // 2 * channels) % (16 * n) == 0
+        lax.axis_size("lat") == 2 and cols == COLS and n * COLS == 128 and rows % 8 == 0
+        and kernels == 8 and (kernels // 2 * channels) % (16 * n) == 0
     )
     plan = in_kernel if fits else on_device
     return plan(features, cotangent, weights, basis, polar_kernel, lon_reach)

time: 60.5 us -> 48.7 us (0.80)
  local copies, waits for them, and re-layouts: 7.87 us -> 3.67 us
  other arithmetic: 6.71 us -> 2.6 us
  Pallas kernels: 44.2 us -> 41.4 us
    pallas_call x1, Pallas kernels: 44.2 us -> 41.4 us  [in_kernel(): pl.pallas_call(functools.partial(fused, n), out_shape=(jax.ShapeDtypeStru...]
    slice x13 -> x0, local copies, waits for them, and re-layouts: 2.41 us -> none  [the longest x4 1.46 us: in_kernel(): quad = jnp.stack([longer[q:q + lat_rows - 1:2] for q in range(4)], 2)]
    another operation x4 -> x0, other arithmetic: 2.22 us -> none
    select_n x3 -> x1, other arithmetic: 2.1 us -> 0.76 us  [in_kernel(): masked = jnp.where(reach_mask[None, :, None, :], basis, 0)]
    unnamed x7 -> x0, other arithmetic: 0.72 us -> none
    le x1, other arithmetic: 0.07 us -> 0.76 us  [in_kernel(): reach_mask = offsets[None, :] <= lon_reach[:, None]]
    transpose x4 -> x0, local copies, waits for them, and re-layouts: 0.68 us -> none  [the longest x1 0.32 us: in_kernel(): quad = jnp.concatenate([quad, edge.swapaxes(0, 1)[None]], 0)]
    another operation x3 -> x0, local copies, waits for them, and re-layouts: 0.68 us -> none
where the time goes in v2:
time: 48.7 us; the launch traced here: 48.4 us
  Pallas kernels  41.4 us (85%)
  local copies, waits for them, and re-layouts  3.67 us (8%)
  other arithmetic  2.6 us (5%)
  between operations  0.68 us (1%)
    pallas_call x1, Pallas kernels, in_kernel(): pl.pallas_call(functools.partial(fused, n), out_shape=(jax.ShapeDtypeStru...  41.4 us
    unnamed x11, local copies, waits for them, and re-layouts  3.44 us
    reshape x1, other arithmetic, in_kernel(): grad_weights.astype(f32).reshape(kernels // 2, channels, channels)  1.06 us

profile of v2, /device:TPU:28, one launch (start us, length us, event | category | flops | bytes accessed | tf_op | source)
XLA Modules:
  0.0 48.4 jit_solution(345092334499877042)
XLA Ops:
  0.6 0.0 copy-start.1
  0.7 0.8 %broadcast_compare_fusion = pred[16,5]{0,1:T(8,128)(4,1)S(1)} fusion(s32[16]{0:T(128)} %param.12, s32[5]{0:T(128)S(1)} %add_abs_fusion), kind=kLoop, calls=%fused_computation.2 | loop fusion | flops 80 | bytes 164 | tf_op jit(solution)/shard_map/le | solution.py:427
  1.4 0.8 %broadcast_select_fusion = bf16[8,16,3,5]{1,0,3,2:T(8,128)(2,1)S(1)} fusion(bf16[8,16,3,5]{1,0,3,2:T(8,128)(2,1)} %param.10, pred[16,5]{0,1:T(8,128)(4,1)S(1)} %broadcast_compare_fusion), kind=kLoop, calls=%fused_computation.1 | loop fusion | flops 1920 | bytes 7760 | tf_op jit(solution)/shard_map/jit(_where)/select_n | solution.py:428
  2.2 0.1 convert_element_type.9
  2.3 0.0 copy-start.2
  2.3 0.1 copy.10
  2.4 0.0 copy-start.4
  2.4 0.0 copy-done.1
  2.4 0.7 %copy-done.2 = bf16[16,8,256]{2,1,0:T(8,128)(2,1)S(1)} copy-done((bf16[16,8,256]{2,1,0:T(8,128)(2,1)S(1)}, bf16[16,8,256]{2,1,0:T(8,128)(2,1)}, u32[]{:S(2)}) %copy-start.2) | copy-done | bytes 65560
  3.1 0.1 copy-done.4
  3.2 0.0 copy-start
  3.2 1.2 %copy-done = bf16[8,256,256]{2,1,0:T(8,128)(2,1)S(1)} copy-done((bf16[8,256,256]{2,1,0:T(8,128)(2,1)S(1)}, bf16[8,256,256]{2,1,0:T(8,128)(2,1)}, u32[]{:S(2)}) %copy-start) | copy-done | bytes 1048600
  4.4 0.0 copy-start.3
  4.4 0.8 %copy-done.3 = bf16[16,8,256]{2,1,0:T(8,128)(2,1)S(1)} copy-done((bf16[16,8,256]{2,1,0:T(8,128)(2,1)S(1)}, bf16[16,8,256]{2,1,0:T(8,128)(2,1)}, u32[]{:S(2)}) %copy-start.3) | copy-done | bytes 65560
  5.2 41.4 %shard_map.86 = (bf16[128,256]{1,0:T(8,128)(2,1)S(1)}, bf16[1024,256]{1,0:T(8,128)(2,1)S(1)}) custom-call(bf16[128,256]{1,0:T(8,128)(2,1)S(1)} %bitcast.11, bf16[128,256]{1,0:T(8,128)(2,1)S(1)} %bitcast.12, bf16[8,256,256]{2,1,0:T(8,128)(2,1)S(1)} %copy-done, f32[128,128]{1,0:T(8,128)S(1)} %pad_convert_fusion.m_ref, f32[64,128]{1,0:T(8,128)S(1)} %bitcast.14, ...), custom_call_target="tpu_custom_call" | custom-call | tf_op jit(solution)/shard_map/pallas_call | solution.py:436
  46.7 1.1 %convert.4 = f32[4,256,256]{2,1,0:T(8,128)} convert(bf16[4,256,256]{2,1,0:T(8,128)(2,1)S(1)} %bitcast.10) | non-fusion elementwise | flops 262144 | bytes 1572864 | tf_op jit(solution)/shard_map/reshape | solution.py:477
  47.7 0.6 %copy.12 = bf16[16,8,256]{2,1,0:T(8,128)(2,1)} copy(bf16[16,8,256]{2,1,0:T(8,128)(2,1)S(1)} %bitcast.13) | data formatting | bytes 131072
  (2 shorter events, 0.0 us)
Async XLA Ops:
  0.6 1.8 %copy-start.1 = (bf16[16,4096]{1,0:T(8,128)(2,1)S(1)}, bf16[16,4096]{1,0:T(8,128)(2,1)}, u32[]{:S(2)}) copy-start(bf16[16,4096]{1,0:T(8,128)(2,1)} %constant.10.clone.d_ref) | copy-start | bytes 393220
  2.3 0.8 %copy-start.2 = (bf16[16,8,256]{2,1,0:T(8,128)(2,1)S(1)}, bf16[16,8,256]{2,1,0:T(8,128)(2,1)}, u32[]{:S(2)}) copy-start(bf16[16,8,256]{2,1,0:T(8,128)(2,1)} %param.7) | copy-start | bytes 196612
  2.4 0.8 %copy-start.4 = (f32[8,2,2,2,128]{4,3,2,1,0:T(2,128)S(1)}, f32[8,2,2,2,128]{4,3,2,1,0:T(2,128)}, u32[]{:S(2)}) copy-start(f32[8,2,2,2,128]{4,3,2,1,0:T(2,128)} %param.11) | copy-start | bytes 98308
  3.2 1.2 %copy-start = (bf16[8,256,256]{2,1,0:T(8,128)(2,1)S(1)}, bf16[8,256,256]{2,1,0:T(8,128)(2,1)}, u32[]{:S(2)}) copy-start(bf16[8,256,256]{2,1,0:T(8,128)(2,1)} %w_ref.1) | copy-start | bytes 3145732
  4.4 0.8 %copy-start.3 = (bf16[16,8,256]{2,1,0:T(8,128)(2,1)S(1)}, bf16[16,8,256]{2,1,0:T(8,128)(2,1)}, u32[]{:S(2)}) copy-start(bf16[16,8,256]{2,1,0:T(8,128)(2,1)} %param.8) | copy-start | bytes 196612

commit v3 on v2

--- a/solution.py
+++ b/solution.py
@@ -147,6 +147,7 @@
     return (interior.astype(jnp.bfloat16), grad_weights)
 
 
+GROUP = 4
 COLS = 8
 SLOTS = 32
 MESH = pl.DeviceIdType.MESH
@@ -179,11 +180,13 @@
 
 
 def fused(
-    n, f_ref, c_ref, w_ref, m_ref, h_ref, d_ref, gf_ref, gw_ref,
+    n, f_ref, c_ref, w_hbm, m_ref, reach_ref, h_ref, d_hbm, gf_ref, gw_ref,
+    w_ref, d_ref, load_sem, basis_in,
     fc, polar, packs, sides, below, rims, near, taps_f, taps_b, rev, circ, ext, sums, own,
-    sib_out, sib_in, part, terms, mine, acc,
+    sib_out, sib_in, part, plane_terms, plane_sums, line_terms, mine, acc,
     send_polar, recv_polar, send_misc, recv_misc, send_sib, recv_sib,
-    send_rs, recv_rs, send_ag, recv_ag,
+    send_plane, recv_plane, send_line, recv_line,
+    send_copy, recv_copy, send_first, recv_first,
 ):
     f32, bf16 = jnp.float32, jnp.bfloat16
     lat, lon = lax.axis_index("lat"), lax.axis_index("lon")
@@ -191,6 +194,7 @@
     rows = points // COLS
     pairs = rows // 2
     kernels = w_ref.shape[0]
+    lines = n // GROUP
     half_k = kernels // 2
     chunk = half_k * channels // n
     window = 4 * SLOTS
@@ -201,6 +205,12 @@
     def turn(t):
         return lax.rem(lon + t, n)
 
+    loads = [
+        pltpu.make_async_copy(src, dst, load_sem.at[i])
+        for i, (src, dst) in enumerate(((d_hbm, d_ref), (w_hbm, w_ref)))
+    ]
+    for load in loads:
+        load.start()
     barrier = pltpu.get_barrier_semaphore()
     for t in range(1, n):
         pl.semaphore_signal(barrier, inc=1, device_id=(lat, turn(t)), device_id_type=MESH)
@@ -223,7 +233,15 @@
                     block = jnp.where(place == u, pltpu.roll(row, shift % COLS, 0), block)
                 packed.append(block)
             packs[side, field] = jnp.concatenate(packed, 0).astype(bf16)
-    by_row = [m_ref[pl.ds(i, kernels, stride=rows), :] for i in range(rows)]
+    span = 2 * REACH + 1
+    basis_in[...] = jnp.zeros_like(basis_in)
+    basis_in[:, : 3 * span] = m_ref[...].astype(f32)
+    lane = lax.broadcasted_iota(jnp.int32, (kernels, 128), 1)
+    away = jnp.abs(lax.rem(lane, span) - REACH)
+    by_row = [
+        jnp.where(away <= reach_ref[i], basis_in[pl.ds(i, kernels, stride=rows), :], 0.0)
+        for i in range(rows)
+    ]
     rims[...] = jnp.where(north, by_row[-1], by_row[0])
     pl.semaphore_wait(barrier, n + 2)
 
@@ -236,8 +254,8 @@
 
     pole_at = pl.multiple_of(lat * (points - 16), 16)
     edge_at = pl.multiple_of(other * (points - 16), 16)
-    arriving = []
-    for field in range(2):
+
+    def send_field(field):
         edge = fc.at[field, pl.ds(edge_at, 16)]
         pole = fc.at[field, pl.ds(pole_at, 16)]
         copies = []
@@ -257,10 +275,11 @@
         )
         for r, (src, dst, to) in enumerate(routes):
             copies.append(push(src, dst, send_misc.at[field, r], recv_misc.at[field, r], to))
-        arriving.append(copies)
         polar[field, 0] = fc[field, pl.ds(pole_at, 16)]
-    arriving[1].append(push(rims, near, send_misc.at[0, 5], recv_misc.at[0, 5], (other, lon)))
-
+        return copies
+
+    field_copies = send_field(0)
+    loads[0].wait()
     mat = jnp.concatenate(by_row, 0)
     taps_f[...] = mul(mat[:, :16].astype(bf16), d_ref[:, :lanes]).astype(bf16).astype(f32)
     zonal = [
@@ -299,8 +318,10 @@
         ext[field, pl.ds((rows + 1) * SLOTS, SLOTS)] = jnp.concatenate([bottom, zeros], 0).astype(bf16)
         return jnp.concatenate(pole_rows, 0).astype(bf16)
 
-    for copy in arriving[0]:
+    for copy in field_copies:
         copy.wait()
+    cotangent_copies = send_field(1)
+    cotangent_copies.append(push(rims, near, send_misc.at[0, 5], recv_misc.at[0, 5], (other, lon)))
     poles = extend(0)
     polar_part = mul(high, poles) + mul(low, poles)
     for p in range(pairs):
@@ -324,37 +345,47 @@
         cells = [sums[h, pl.ds(k, points, stride=kernels), :] for h in range(channels // 128)]
         return mul(jnp.concatenate(cells, 1).astype(bf16), cot, ((0,), (0,)))
 
-    to_sib = []
-    for j in range(half_k):
-        at = pl.ds(j * channels, channels)
-        sib_out[at] = gradient(other * half_k + j).astype(bf16)
-        to_sib.append(
-            push(sib_out.at[at], sib_in.at[at], send_sib.at[j], recv_sib.at[j], (other, lon))
-        )
-    for j in range(half_k):
-        own[pl.ds(j * channels, channels)] = gradient(lat * half_k + j)
-    for j in range(half_k):
-        at = pl.ds(j * channels, channels)
-        to_sib[j].wait()
-        part[at] = (own[at] + sib_in[at].astype(f32)).astype(bf16)
-    scatter = []
-    for t in range(1, n):
-        at = pl.ds(pl.multiple_of(turn(t) * chunk, chunk), chunk)
-        scatter.append(
-            push(part.at[at], terms.at[t], send_rs.at[t], recv_rs.at[t], (lat, turn(t)))
-        )
-
-    for copy in arriving[1]:
-        copy.wait()
-    poles = extend(1)
+    line, spot = lon // GROUP, lax.rem(lon, GROUP)
+
+    def in_plane(t):
+        return (lat, line * GROUP + lax.rem(spot + t, GROUP))
+
+    def on_line(t):
+        return (lat, lax.rem(line + t, lines) * GROUP + spot)
+
+    def rows_of(line_at, spot_at):
+        return pl.ds(pl.multiple_of((line_at * GROUP + spot_at) * chunk, chunk), chunk)
+
+    order = list(range(1, lines)) + [0]
+    to_sib = {}
+    for t in order:
+        j = lax.rem(line + t, lines)
+        sib_out[t] = gradient(other * half_k + j).astype(bf16)
+        to_sib[t] = push(sib_out.at[t], sib_in.at[t], send_sib.at[t], recv_sib.at[t], (other, lon))
+    for t in order:
+        own[t] = gradient(lat * half_k + lax.rem(line + t, lines))
+    plane = {}
+    for t in order:
+        j = lax.rem(line + t, lines)
+        to_sib[t].wait()
+        part[pl.ds(pl.multiple_of(j * channels, channels), channels)] = (
+            own[t] + sib_in[t].astype(f32)
+        ).astype(bf16)
+        plane[t] = [
+            push(
+                part.at[rows_of(j, lax.rem(spot + u, GROUP))], plane_terms.at[u, t],
+                send_plane.at[u, t], recv_plane.at[u, t], in_plane(u),
+            )
+            for u in range(1, GROUP)
+        ]
     taps_each = 3 * (2 * REACH + 1)
     step = 2 * (2 * REACH + 1)
-    lane = lax.broadcasted_iota(jnp.int32, (kernels, 128), 1)
     first_taps = lane < taps_each - step
     up = jnp.where(first_taps, by_row[0], 0.0)
     up = pltpu.roll(up, step, 1)
     down = pltpu.roll(by_row[-1], 128 - step, 1)
     down = jnp.where(first_taps, down, 0.0)
+    cotangent_copies[-1].wait()
     beside = near[...]
     mat = jnp.concatenate(
         [jnp.where(north, up, beside)] + by_row + [jnp.where(north, beside, down)], 0
@@ -383,7 +414,23 @@
         for j in range(COLS):
             for a in range(2):
                 circ[a, pl.ds((r * COLS + j) * kernels, kernels)] = pltpu.roll(turned[a], j + 1, 1)
+    along = {}
+    for t in order:
+        total = part[rows_of(lax.rem(line + t, lines), spot)].astype(f32)
+        for u in range(1, GROUP):
+            plane[t][u - 1].wait()
+            total = total + plane_terms[u, t].astype(f32)
+        if t:
+            plane_sums[t] = total.astype(bf16)
+            along[t] = push(
+                plane_sums.at[t], line_terms.at[t], send_line.at[t], recv_line.at[t], on_line(t)
+            )
+
     acc[...] = jnp.zeros_like(acc)
+    for copy in cotangent_copies[:-1]:
+        copy.wait()
+    poles = extend(1)
+    loads[1].wait()
 
     def per_kernel(k, pole_acc):
         weight = w_ref[k]
@@ -402,16 +449,28 @@
     acc[pl.ds(points - 16, 16)] += jnp.where(north, 0.0, pole_acc)
     gf_ref[...] = acc[...].astype(bf16)
 
-    here = pl.ds(pl.multiple_of(lon * chunk, chunk), chunk)
-    total = part[here].astype(f32)
-    for t in range(1, n):
-        scatter[t - 1].wait()
-        total = total + terms[t].astype(f32)
+    here = rows_of(line, spot)
+    for t in range(1, lines):
+        along[t].wait()
+        total = total + line_terms[t].astype(f32)
     mine[...] = total.astype(bf16)
     gw_ref[here] = mine[...]
-    gather = []
-    for t in range(1, n):
-        gather.append(push(mine, gw_ref.at[here], send_ag.at[t], recv_ag.at[t], (lat, turn(t))))
+
+    def spread_plane(src, at, t):
+        return [
+            push(src, gw_ref.at[at], send_copy.at[u, t], recv_copy.at[u, t], in_plane(u))
+            for u in range(1, GROUP)
+        ]
+
+    first = [
+        push(mine, gw_ref.at[here], send_first.at[t], recv_first.at[t], on_line(t))
+        for t in range(1, lines)
+    ]
+    gather = spread_plane(mine, here, 0)
+    for t in range(1, lines):
+        first[t - 1].wait()
+        at = rows_of(lax.rem(line - t + lines, lines), spot)
+        gather += spread_plane(gw_ref.at[at], at, t)
     for copy in gather:
         copy.wait()
 
@@ -423,25 +482,27 @@
     pairs, points = lat_rows // 2, lat_rows * lon_cols
     taps = 3 * (2 * REACH + 1)
     bf16, f32 = jnp.bfloat16, jnp.float32
-    offsets = jnp.abs(jnp.arange(2 * REACH + 1, dtype=jnp.int32) - REACH)
-    reach_mask = offsets[None, :] <= lon_reach[:, None]
-    masked = jnp.where(reach_mask[None, :, None, :], basis, 0)
-    masked = masked.reshape(kernels * lat_rows, taps).astype(f32)
-    masked = jnp.pad(masked, ((0, 0), (0, 128 - taps)))
+    masked = basis.reshape(kernels * lat_rows, taps)
     spread = jnp.asarray(spread_matrices(), bf16)
     half = kernels * channels // 2
     window, pack = 4 * SLOTS, lat_rows * REACH
     dma = pltpu.SemaphoreType.DMA
     vmem = pl.BlockSpec(memory_space=pltpu.VMEM)
+    hbm = pl.BlockSpec(memory_space=pl.ANY)
+    lines = n // GROUP
     grad_features, grad_weights = pl.pallas_call(
         functools.partial(fused, n),
         out_shape=(
             jax.ShapeDtypeStruct((points, channels), bf16),
             jax.ShapeDtypeStruct((half, channels), bf16),
         ),
-        in_specs=[vmem] * 6,
+        in_specs=[vmem, vmem, hbm, vmem, pl.BlockSpec(memory_space=pltpu.SMEM), vmem, hbm],
         out_specs=(vmem, vmem),
         scratch_shapes=[
+            pltpu.VMEM(weights.shape, bf16),
+            pltpu.VMEM(spread.shape, bf16),
+            dma((2,)),
+            pltpu.VMEM((kernels * lat_rows, 128), f32),
             pltpu.VMEM((2, points, channels), bf16),
             pltpu.VMEM((2, n, 16, channels), bf16),
             pltpu.VMEM((2, 2, pack, channels), bf16),
@@ -455,22 +516,25 @@
             pltpu.VMEM((2, 16 * kernels, lon_cols * n), f32),
             pltpu.VMEM((2, (lat_rows + 2) * SLOTS, channels), bf16),
             pltpu.VMEM((channels // 128, points * kernels, 128), f32),
-            pltpu.VMEM((half, channels), f32),
+            pltpu.VMEM((lines, channels, channels), f32),
+            pltpu.VMEM((lines, channels, channels), bf16),
+            pltpu.VMEM((lines, channels, channels), bf16),
             pltpu.VMEM((half, channels), bf16),
-            pltpu.VMEM((half, channels), bf16),
-            pltpu.VMEM((half, channels), bf16),
-            pltpu.VMEM((n, half // n, channels), bf16),
+            pltpu.VMEM((GROUP, lines, half // n, channels), bf16),
+            pltpu.VMEM((lines, half // n, channels), bf16),
+            pltpu.VMEM((lines, half // n, channels), bf16),
             pltpu.VMEM((half // n, channels), bf16),
             pltpu.VMEM((points, channels), f32),
             dma((2, n)), dma((2, n)), dma((2, 6)), dma((2, 6)), dma((4,)), dma((4,)),
-            dma((n,)), dma((n,)), dma((n,)), dma((n,)),
+            dma((GROUP, lines)), dma((GROUP, lines)), dma((lines,)), dma((lines,)),
+            dma((GROUP, lines)), dma((GROUP, lines)), dma((lines,)), dma((lines,)),
         ],
         compiler_params=pltpu.CompilerParams(
-            collective_id=0, has_side_effects=True, vmem_limit_bytes=40 * 2**20
+            collective_id=0, has_side_effects=True, vmem_limit_bytes=56 * 2**20
         ),
     )(
         features.reshape(points, channels), cotangent.reshape(points, channels),
-        weights, masked, polar_kernel.reshape(kernels * 8, lon_cols * n), spread,
+        weights, masked, lon_reach, polar_kernel.reshape(kernels * 8, lon_cols * n), spread,
     )
     return (
         grad_features.reshape(features.shape),
@@ -483,7 +547,7 @@
     n = lax.axis_size("lon")
     kernels = weights.shape[0]
     fits = (
-        lax.axis_size("lat") == 2 and cols == COLS and n * COLS == 128 and rows % 8 == 0
+        lax.axis_size("lat") == 2 and cols == COLS and n * COLS == 128 and n == GROUP * (kernels // 2) and rows % 8 == 0
         and kernels == 8 and (kernels // 2 * channels) % (16 * n) == 0
     )
     plan = in_kernel if fits else on_device

time: 48.7 us -> 46.4 us (0.953)
  the two profiles are of different devices: /device:TPU:28 before, /device:TPU:0 now
where the time goes in v3:
time: 46.4 us; the launch traced here: 46.2 us
  Pallas kernels  41.2 us (89%)
  local copies, waits for them, and re-layouts  2.22 us (5%)
  other arithmetic  2.13 us (5%)
  between operations  0.65 us (1%)
    pallas_call x1, Pallas kernels, in_kernel(): pl.pallas_call(functools.partial(fused, n), out_shape=(jax.ShapeDtypeStru...  41.2 us
    reshape x1, other arithmetic, in_kernel(): grad_weights.astype(f32).reshape(kernels // 2, channels, channels)  2.13 us
    reshape x2, local copies, waits for them, and re-layouts, in_kernel(): masked = basis.reshape(kernels * lat_rows, taps)  1.58 us

profile of v3, /device:TPU:0, one launch (start us, length us, event | category | flops | bytes accessed | tf_op | source)
XLA Modules:
  0.0 46.2 jit_solution(6473592294855123104)
XLA Ops:
  0.6 0.8 %reshape.27 = bf16[128,15]{0,1:T(8,128)(2,1)S(1)} reshape(bf16[8,16,3,5]{1,0,3,2:T(8,128)(2,1)} %param.10) | data formatting | bytes 7680 | tf_op jit(solution)/shard_map/reshape | solution.py:485
  1.5 0.7 %copy.10.m_ref = bf16[128,15]{1,0:T(8,128)(2,1)} copy(bf16[128,15]{0,1:T(8,128)(2,1)S(1)} %reshape.27) | data formatting | bytes 7680 | tf_op jit(solution)/shard_map/reshape | solution.py:485
  2.2 41.2 %shard_map.86 = (bf16[128,256]{1,0:T(8,128)(2,1)}, bf16[1024,256]{1,0:T(8,128)(2,1)}) custom-call(bf16[128,256]{1,0:T(8,128)(2,1)} %bitcast.11, bf16[128,256]{1,0:T(8,128)(2,1)} %bitcast.12, bf16[8,256,256]{2,1,0:T(8,128)(2,1)} %w_hbm.1, bf16[128,15]{1,0:T(8,128)(2,1)} %copy.10.m_ref, s32[16]{0:T(128)} %reach_ref.1, f32[64,128]{1,0:T(8,128)} %bitcast.14, ...), custom_call_target="tpu_custom_call" | custom-call | tf_op jit(solution)/shard_map/pallas_call | solution.py:493
  43.4 0.0 copy-start
  43.4 2.1 %convert.1 = f32[4,256,256]{2,1,0:T(8,128)} convert(bf16[4,256,256]{2,1,0:T(8,128)(2,1)} %bitcast.10) | non-fusion elementwise | flops 262144 | bytes 1572864 | tf_op jit(solution)/shard_map/reshape | solution.py:541
  45.5 0.0 copy-done
  45.5 0.6 %copy.12 = bf16[16,8,256]{2,1,0:T(8,128)(2,1)} copy(bf16[16,8,256]{2,1,0:T(8,128)(2,1)S(1)} %bitcast.13) | data formatting | bytes 131072
Async XLA Ops:
  43.4 2.1 %copy-start = (bf16[128,256]{1,0:T(8,128)(2,1)S(1)}, bf16[128,256]{1,0:T(8,128)(2,1)}, u32[]{:S(2)}) copy-start(bf16[128,256]{1,0:T(8,128)(2,1)} %get-tuple-element.4) | copy-start | bytes 196612

commit v4 on v3

--- a/solution.py
+++ b/solution.py
@@ -180,8 +180,8 @@
 
 
 def fused(
-    n, f_ref, c_ref, w_hbm, m_ref, reach_ref, h_ref, d_hbm, gf_ref, gw_ref,
-    w_ref, d_ref, load_sem, basis_in,
+    n, f_hbm, c_hbm, w_hbm, m_hbm, reach_ref, h_hbm, d_hbm, gf_ref, gw_ref,
+    w_ref, m_ref, h_ref, d_ref, load_sem, basis_in,
     fc, polar, packs, sides, below, rims, near, taps_f, taps_b, rev, circ, ext, sums, own,
     sib_out, sib_in, part, plane_terms, plane_sums, line_terms, mine, acc,
     send_polar, recv_polar, send_misc, recv_misc, send_sib, recv_sib,
@@ -190,7 +190,7 @@
 ):
     f32, bf16 = jnp.float32, jnp.bfloat16
     lat, lon = lax.axis_index("lat"), lax.axis_index("lon")
-    points, channels = f_ref.shape
+    points, channels = f_hbm.shape
     rows = points // COLS
     pairs = rows // 2
     kernels = w_ref.shape[0]
@@ -205,20 +205,22 @@
     def turn(t):
         return lax.rem(lon + t, n)
 
-    loads = [
-        pltpu.make_async_copy(src, dst, load_sem.at[i])
-        for i, (src, dst) in enumerate(((d_hbm, d_ref), (w_hbm, w_ref)))
-    ]
-    for load in loads:
-        load.start()
     barrier = pltpu.get_barrier_semaphore()
     for t in range(1, n):
         pl.semaphore_signal(barrier, inc=1, device_id=(lat, turn(t)), device_id_type=MESH)
     for t in (0, 1, n - 1):
         pl.semaphore_signal(barrier, inc=1, device_id=(other, turn(t)), device_id_type=MESH)
 
-    fc[0] = f_ref[...]
-    fc[1] = c_ref[...]
+    sources = (f_hbm, c_hbm, m_hbm, d_hbm, h_hbm, w_hbm)
+    places = (fc.at[0], fc.at[1], m_ref, d_ref, h_ref, w_ref)
+    loads = [
+        pltpu.make_async_copy(src, dst, load_sem.at[i])
+        for i, (src, dst) in enumerate(zip(sources, places))
+    ]
+    for load in loads:
+        load.start()
+    for load in loads[:3]:
+        load.wait()
     place = lax.broadcasted_iota(jnp.int32, (COLS, channels), 0) // REACH
     group = COLS // REACH
     for field in range(2):
@@ -279,7 +281,8 @@
         return copies
 
     field_copies = send_field(0)
-    loads[0].wait()
+    loads[3].wait()
+    loads[4].wait()
     mat = jnp.concatenate(by_row, 0)
     taps_f[...] = mul(mat[:, :16].astype(bf16), d_ref[:, :lanes]).astype(bf16).astype(f32)
     zonal = [
@@ -318,6 +321,19 @@
         ext[field, pl.ds((rows + 1) * SLOTS, SLOTS)] = jnp.concatenate([bottom, zeros], 0).astype(bf16)
         return jnp.concatenate(pole_rows, 0).astype(bf16)
 
+    flip = lax.broadcasted_iota(jnp.int32, (128, 128), 0) + lax.broadcasted_iota(
+        jnp.int32, (128, 128), 1
+    )
+    flip = jnp.where(flip == 127, 1.0, 0.0).astype(bf16)
+    flip_high, flip_low = split(h_ref[...])
+    rev[...] = mul(flip_high, flip) + mul(flip_low, flip)
+    for r in range(2):
+        turned = [
+            rev[pl.ds(lat * 4 + a * 2 + r, kernels, stride=8), :] for a in range(2)
+        ]
+        for j in range(COLS):
+            for a in range(2):
+                circ[a, pl.ds((r * COLS + j) * kernels, kernels)] = pltpu.roll(turned[a], j + 1, 1)
     for copy in field_copies:
         copy.wait()
     cotangent_copies = send_field(1)
@@ -339,7 +355,7 @@
         for h in range(channels // 128):
             sums[h, pl.ds(16 * kernels * p, 16 * kernels)] = value[:, 128 * h : 128 * (h + 1)]
 
-    cot = c_ref[...]
+    cot = fc[1]
 
     def gradient(k):
         cells = [sums[h, pl.ds(k, points, stride=kernels), :] for h in range(channels // 128)]
@@ -401,19 +417,6 @@
                     part_of == q, spread[i : i + kernels, x * window : (x + 1) * window], tile
                 )
             taps_b[pl.ds((16 * p + x) * kernels, kernels)] = tile
-    flip = lax.broadcasted_iota(jnp.int32, (128, 128), 0) + lax.broadcasted_iota(
-        jnp.int32, (128, 128), 1
-    )
-    flip = jnp.where(flip == 127, 1.0, 0.0).astype(bf16)
-    high, low = split(h_ref[...])
-    rev[...] = mul(high, flip) + mul(low, flip)
-    for r in range(2):
-        turned = [
-            rev[pl.ds(lat * 4 + a * 2 + r, kernels, stride=8), :] for a in range(2)
-        ]
-        for j in range(COLS):
-            for a in range(2):
-                circ[a, pl.ds((r * COLS + j) * kernels, kernels)] = pltpu.roll(turned[a], j + 1, 1)
     along = {}
     for t in order:
         total = part[rows_of(lax.rem(line + t, lines), spot)].astype(f32)
@@ -430,7 +433,7 @@
     for copy in cotangent_copies[:-1]:
         copy.wait()
     poles = extend(1)
-    loads[1].wait()
+    loads[5].wait()
 
     def per_kernel(k, pole_acc):
         weight = w_ref[k]
@@ -444,11 +447,8 @@
         )
         return pole_acc + mul(high, pole_grad) + mul(low, pole_grad)
 
-    pole_acc = lax.fori_loop(0, kernels, per_kernel, jnp.zeros((16, channels), f32))
-    acc[pl.ds(0, 16)] += jnp.where(north, pole_acc, 0.0)
-    acc[pl.ds(points - 16, 16)] += jnp.where(north, 0.0, pole_acc)
-    gf_ref[...] = acc[...].astype(bf16)
-
+    pole_acc = jnp.zeros((16, channels), f32)
+    pole_acc = lax.fori_loop(0, 3, per_kernel, pole_acc)
     here = rows_of(line, spot)
     for t in range(1, lines):
         along[t].wait()
@@ -462,15 +462,23 @@
             for u in range(1, GROUP)
         ]
 
-    first = [
-        push(mine, gw_ref.at[here], send_first.at[t], recv_first.at[t], on_line(t))
-        for t in range(1, lines)
-    ]
+    near_first = sorted(range(1, lines), key=lambda t: min(t, lines - t))
+    first = {
+        t: push(mine, gw_ref.at[here], send_first.at[t], recv_first.at[t], on_line(t))
+        for t in near_first
+    }
     gather = spread_plane(mine, here, 0)
-    for t in range(1, lines):
-        first[t - 1].wait()
+    done = 3
+    for t in near_first:
+        pole_acc = per_kernel(done, pole_acc)
+        done += 1
+        first[t].wait()
         at = rows_of(lax.rem(line - t + lines, lines), spot)
         gather += spread_plane(gw_ref.at[at], at, t)
+    pole_acc = lax.fori_loop(done, kernels, per_kernel, pole_acc)
+    acc[pl.ds(0, 16)] += jnp.where(north, pole_acc, 0.0)
+    acc[pl.ds(points - 16, 16)] += jnp.where(north, 0.0, pole_acc)
+    gf_ref[...] = acc[...].astype(bf16)
     for copy in gather:
         copy.wait()
 
@@ -488,7 +496,7 @@
     window, pack = 4 * SLOTS, lat_rows * REACH
     dma = pltpu.SemaphoreType.DMA
     vmem = pl.BlockSpec(memory_space=pltpu.VMEM)
-    hbm = pl.BlockSpec(memory_space=pl.ANY)
+    hbm = pl.BlockSpec(memory_space=pltpu.HBM)
     lines = n // GROUP
     grad_features, grad_weights = pl.pallas_call(
         functools.partial(fused, n),
@@ -496,12 +504,14 @@
             jax.ShapeDtypeStruct((points, channels), bf16),
             jax.ShapeDtypeStruct((half, channels), bf16),
         ),
-        in_specs=[vmem, vmem, hbm, vmem, pl.BlockSpec(memory_space=pltpu.SMEM), vmem, hbm],
+        in_specs=[hbm] * 4 + [pl.BlockSpec(memory_space=pltpu.SMEM)] + [hbm] * 2,
         out_specs=(vmem, vmem),
         scratch_shapes=[
             pltpu.VMEM(weights.shape, bf16),
+            pltpu.VMEM(masked.shape, bf16),
+            pltpu.VMEM((kernels * 8, lon_cols * n), f32),
             pltpu.VMEM(spread.shape, bf16),
-            dma((2,)),
+            dma((6,)),
             pltpu.VMEM((kernels * lat_rows, 128), f32),
             pltpu.VMEM((2, points, channels), bf16),
             pltpu.VMEM((2, n, 16, channels), bf16),

time: 46.4 us -> 42.5 us (0.916)
  Pallas kernels: 41.2 us -> 37.3 us
    pallas_call x1, Pallas kernels: 41.2 us -> 37.3 us  [in_kernel(): pl.pallas_call(functools.partial(fused, n), out_shape=(jax.ShapeDtypeStru...]
where the time goes in v4:
time: 42.5 us; the launch traced here: 42.3 us
  Pallas kernels  37.3 us (88%)
  local copies, waits for them, and re-layouts  2.22 us (5%)
  other arithmetic  2.13 us (5%)
  between operations  0.65 us (2%)
    pallas_call x1, Pallas kernels, in_kernel(): pl.pallas_call(functools.partial(fused, n), out_shape=(jax.ShapeDtypeStru...  37.3 us
    reshape x1, other arithmetic, in_kernel(): grad_weights.astype(f32).reshape(kernels // 2, channels, channels)  2.13 us
    reshape x2, local copies, waits for them, and re-layouts, in_kernel(): masked = basis.reshape(kernels * lat_rows, taps)  1.58 us

profile of v4, /device:TPU:0, one launch (start us, length us, event | category | flops | bytes accessed | tf_op | source)
XLA Modules:
  0.0 42.3 jit_solution(15717795189472172424)
XLA Ops:
  0.6 0.8 %reshape.27 = bf16[128,15]{0,1:T(8,128)(2,1)S(1)} reshape(bf16[8,16,3,5]{1,0,3,2:T(8,128)(2,1)} %param.10) | data formatting | bytes 7680 | tf_op jit(solution)/shard_map/reshape | solution.py:493
  1.5 0.7 %copy.10.m_hbm = bf16[128,15]{1,0:T(8,128)(2,1)} copy(bf16[128,15]{0,1:T(8,128)(2,1)S(1)} %reshape.27) | data formatting | bytes 7680 | tf_op jit(solution)/shard_map/reshape | solution.py:493
  2.2 37.3 %shard_map.86 = (bf16[128,256]{1,0:T(8,128)(2,1)}, bf16[1024,256]{1,0:T(8,128)(2,1)}) custom-call(bf16[128,256]{1,0:T(8,128)(2,1)} %bitcast.11, bf16[128,256]{1,0:T(8,128)(2,1)} %bitcast.12, bf16[8,256,256]{2,1,0:T(8,128)(2,1)} %w_hbm.1, bf16[128,15]{1,0:T(8,128)(2,1)} %copy.10.m_hbm, s32[16]{0:T(128)} %reach_ref.1, f32[64,128]{1,0:T(8,128)} %bitcast.14, ...), custom_call_target="tpu_custom_call" | custom-call | tf_op jit(solution)/shard_map/pallas_call | solution.py:501
  39.5 0.0 copy-start
  39.5 2.1 %convert.1 = f32[4,256,256]{2,1,0:T(8,128)} convert(bf16[4,256,256]{2,1,0:T(8,128)(2,1)} %bitcast.10) | non-fusion elementwise | flops 262144 | bytes 1572864 | tf_op jit(solution)/shard_map/reshape | solution.py:551
  41.6 0.0 copy-done
  41.6 0.6 %copy.12 = bf16[16,8,256]{2,1,0:T(8,128)(2,1)} copy(bf16[16,8,256]{2,1,0:T(8,128)(2,1)S(1)} %bitcast.13) | data formatting | bytes 131072
Async XLA Ops:
  39.5 2.1 %copy-start = (bf16[128,256]{1,0:T(8,128)(2,1)S(1)}, bf16[128,256]{1,0:T(8,128)(2,1)}, u32[]{:S(2)}) copy-start(bf16[128,256]{1,0:T(8,128)(2,1)} %get-tuple-element.4) | copy-start | bytes 196612

commit v5 on v4

--- a/solution.py
+++ b/solution.py
@@ -181,7 +181,7 @@
 
 def fused(
     n, f_hbm, c_hbm, w_hbm, m_hbm, reach_ref, h_hbm, d_hbm, gf_ref, gw_ref,
-    w_ref, m_ref, h_ref, d_ref, load_sem, basis_in,
+    w_ref, m_ref, h_ref, d_ref, load_sem, basis_in, basis_by_row,
     fc, polar, packs, sides, below, rims, near, taps_f, taps_b, rev, circ, ext, sums, own,
     sib_out, sib_in, part, plane_terms, plane_sums, line_terms, mine, acc,
     send_polar, recv_polar, send_misc, recv_misc, send_sib, recv_sib,
@@ -237,11 +237,19 @@
             packs[side, field] = jnp.concatenate(packed, 0).astype(bf16)
     span = 2 * REACH + 1
     basis_in[...] = jnp.zeros_like(basis_in)
-    basis_in[:, : 3 * span] = m_ref[...].astype(f32)
+    basis_in[: 3 * span * kernels, :rows] = m_ref[...].astype(f32)
+    unit = lax.broadcasted_iota(jnp.int32, (16, 128), 0) == lax.broadcasted_iota(
+        jnp.int32, (16, 128), 1
+    )
+    unit = jnp.where(unit, 1.0, 0.0).astype(bf16)
+    for k in range(kernels):
+        by_tap = basis_in[pl.ds(k, 16, stride=kernels), :].astype(bf16)
+        flipped = mul(by_tap, unit, ((0,), (0,)))
+        basis_by_row[pl.ds(k * rows, rows)] = flipped[:rows]
     lane = lax.broadcasted_iota(jnp.int32, (kernels, 128), 1)
     away = jnp.abs(lax.rem(lane, span) - REACH)
     by_row = [
-        jnp.where(away <= reach_ref[i], basis_in[pl.ds(i, kernels, stride=rows), :], 0.0)
+        jnp.where(away <= reach_ref[i], basis_by_row[pl.ds(i, kernels, stride=rows), :], 0.0)
         for i in range(rows)
     ]
     rims[...] = jnp.where(north, by_row[-1], by_row[0])
@@ -490,7 +498,7 @@
     pairs, points = lat_rows // 2, lat_rows * lon_cols
     taps = 3 * (2 * REACH + 1)
     bf16, f32 = jnp.bfloat16, jnp.float32
-    masked = basis.reshape(kernels * lat_rows, taps)
+    masked = basis.transpose(2, 3, 0, 1).reshape(taps * kernels, lat_rows)
     spread = jnp.asarray(spread_matrices(), bf16)
     half = kernels * channels // 2
     window, pack = 4 * SLOTS, lat_rows * REACH
@@ -512,6 +520,7 @@
             pltpu.VMEM((kernels * 8, lon_cols * n), f32),
             pltpu.VMEM(spread.shape, bf16),
             dma((6,)),
+            pltpu.VMEM((16 * kernels, 128), f32),
             pltpu.VMEM((kernels * lat_rows, 128), f32),
             pltpu.VMEM((2, points, channels), bf16),
             pltpu.VMEM((2, n, 16, channels), bf16),

time: 42.5 us -> 40.9 us (0.962)
  local copies, waits for them, and re-layouts: 2.22 us -> 0.63 us
    reshape x2 -> x0, local copies, waits for them, and re-layouts: 1.58 us -> none  [in_kernel(): masked = basis.reshape(kernels * lat_rows, taps)]
where the time goes in v5:
time: 40.9 us; the launch traced here: 40.7 us
  Pallas kernels  37.3 us (91%)
  other arithmetic  2.13 us (5%)
  between operations  0.65 us (2%)
  local copies, waits for them, and re-layouts  0.63 us (2%)
    pallas_call x1, Pallas kernels, in_kernel(): pl.pallas_call(functools.partial(fused, n), out_shape=(jax.ShapeDtypeStru...  37.3 us
    reshape x1, other arithmetic, in_kernel(): grad_weights.astype(f32).reshape(kernels // 2, channels, channels)  2.13 us

profile of v5, /device:TPU:0, one launch (start us, length us, event | category | flops | bytes accessed | tf_op | source)
XLA Modules:
  0.0 40.7 jit_solution(16552808864731959189)
XLA Ops:
  0.6 37.3 %shard_map.86 = (bf16[128,256]{1,0:T(8,128)(2,1)}, bf16[1024,256]{1,0:T(8,128)(2,1)}) custom-call(bf16[128,256]{1,0:T(8,128)(2,1)} %bitcast.10, bf16[128,256]{1,0:T(8,128)(2,1)} %bitcast.11, bf16[8,256,256]{2,1,0:T(8,128)(2,1)} %w_hbm.1, bf16[120,16]{1,0:T(8,128)(2,1)} %bitcast.14, s32[16]{0:T(128)} %reach_ref.1, f32[64,128]{1,0:T(8,128)} %bitcast.13, ...), custom_call_target="tpu_custom_call" | custom-call | tf_op jit(solution)/shard_map/pallas_call | solution.py:509
  37.9 0.0 copy-start
  37.9 2.1 %convert.1 = f32[4,256,256]{2,1,0:T(8,128)} convert(bf16[4,256,256]{2,1,0:T(8,128)(2,1)} %bitcast.9) | non-fusion elementwise | flops 262144 | bytes 1572864 | tf_op jit(solution)/shard_map/reshape | solution.py:560
  40.1 0.0 copy-done
  40.1 0.6 %copy.10 = bf16[16,8,256]{2,1,0:T(8,128)(2,1)} copy(bf16[16,8,256]{2,1,0:T(8,128)(2,1)S(1)} %bitcast.12) | data formatting | bytes 131072
Async XLA Ops:
  37.9 2.1 %copy-start = (bf16[128,256]{1,0:T(8,128)(2,1)S(1)}, bf16[128,256]{1,0:T(8,128)(2,1)}, u32[]{:S(2)}) copy-start(bf16[128,256]{1,0:T(8,128)(2,1)} %get-tuple-element.4) | copy-start | bytes 196612

commit v6 on v5

--- a/solution.py
+++ b/solution.py
@@ -456,7 +456,7 @@
         return pole_acc + mul(high, pole_grad) + mul(low, pole_grad)
 
     pole_acc = jnp.zeros((16, channels), f32)
-    pole_acc = lax.fori_loop(0, 3, per_kernel, pole_acc)
+    pole_acc = lax.fori_loop(0, 1, per_kernel, pole_acc)
     here = rows_of(line, spot)
     for t in range(1, lines):
         along[t].wait()
@@ -476,7 +476,7 @@
         for t in near_first
     }
     gather = spread_plane(mine, here, 0)
-    done = 3
+    done = 1
     for t in near_first:
         pole_acc = per_kernel(done, pole_acc)
         done += 1

time: 40.9 us -> 40.2 us (0.983)
  Pallas kernels: 37.3 us -> 36.6 us
    pallas_call x1, Pallas kernels: 37.3 us -> 36.6 us  [in_kernel(): pl.pallas_call(functools.partial(fused, n), out_shape=(jax.ShapeDtypeStru...]
where the time goes in v6:
time: 40.2 us; the launch traced here: 40.1 us
  Pallas kernels  36.6 us (91%)
  other arithmetic  2.13 us (5%)
  between operations  0.65 us (2%)
  local copies, waits for them, and re-layouts  0.63 us (2%)
    pallas_call x1, Pallas kernels, in_kernel(): pl.pallas_call(functools.partial(fused, n), out_shape=(jax.ShapeDtypeStru...  36.6 us
    reshape x1, other arithmetic, in_kernel(): grad_weights.astype(f32).reshape(kernels // 2, channels, channels)  2.13 us

profile of v6, /device:TPU:0, one launch (start us, length us, event | category | flops | bytes accessed | tf_op | source)
XLA Modules:
  0.0 40.1 jit_solution(12912270946517951457)
XLA Ops:
  0.6 36.6 %shard_map.86 = (bf16[128,256]{1,0:T(8,128)(2,1)}, bf16[1024,256]{1,0:T(8,128)(2,1)}) custom-call(bf16[128,256]{1,0:T(8,128)(2,1)} %bitcast.10, bf16[128,256]{1,0:T(8,128)(2,1)} %bitcast.11, bf16[8,256,256]{2,1,0:T(8,128)(2,1)} %w_hbm.1, bf16[120,16]{1,0:T(8,128)(2,1)} %bitcast.14, s32[16]{0:T(128)} %reach_ref.1, f32[64,128]{1,0:T(8,128)} %bitcast.13, ...), custom_call_target="tpu_custom_call" | custom-call | tf_op jit(solution)/shard_map/pallas_call | solution.py:509
  37.3 0.0 copy-start
  37.3 2.1 %convert.1 = f32[4,256,256]{2,1,0:T(8,128)} convert(bf16[4,256,256]{2,1,0:T(8,128)(2,1)} %bitcast.9) | non-fusion elementwise | flops 262144 | bytes 1572864 | tf_op jit(solution)/shard_map/reshape | solution.py:560
  39.4 0.0 copy-done
  39.4 0.6 %copy.10 = bf16[16,8,256]{2,1,0:T(8,128)(2,1)} copy(bf16[16,8,256]{2,1,0:T(8,128)(2,1)S(1)} %bitcast.12) | data formatting | bytes 131072
Async XLA Ops:
  37.3 2.1 %copy-start = (bf16[128,256]{1,0:T(8,128)(2,1)S(1)}, bf16[128,256]{1,0:T(8,128)(2,1)}, u32[]{:S(2)}) copy-start(bf16[128,256]{1,0:T(8,128)(2,1)} %get-tuple-element.4) | copy-start | bytes 196612

commit v7 on v6

--- a/solution.py
+++ b/solution.py
@@ -303,9 +303,7 @@
     ]
     high, low = split(jnp.concatenate(rolled, 0))
 
-    def extend(field):
-        gathered = polar[field].astype(f32).reshape(n, 2, COLS, channels)
-        pole_rows = [gathered[:, r].reshape(n * COLS, channels) for r in range(2)]
+    def extend_inside(field):
         zeros = jnp.zeros((COLS, channels), f32)
         left, right = sides[0, field].astype(f32), sides[1, field].astype(f32)
         cells = fc[field].astype(f32)
@@ -319,6 +317,11 @@
                 zeros,
             ]
             ext[field, pl.ds((i + 1) * SLOTS, SLOTS)] = jnp.concatenate(line, 0).astype(bf16)
+
+    def extend_ends(field):
+        gathered = polar[field].astype(f32).reshape(n, 2, COLS, channels)
+        pole_rows = [gathered[:, r].reshape(n * COLS, channels) for r in range(2)]
+        zeros = jnp.zeros((COLS, channels), f32)
         turned = gathered[n // 2 - 1 : n // 2 + 2]
         turned = jnp.where(north, turned[:, 0], turned[:, 1])
         beside = below[field].astype(f32).reshape(3, 2, COLS, channels)
@@ -342,13 +345,7 @@
         for j in range(COLS):
             for a in range(2):
                 circ[a, pl.ds((r * COLS + j) * kernels, kernels)] = pltpu.roll(turned[a], j + 1, 1)
-    for copy in field_copies:
-        copy.wait()
-    cotangent_copies = send_field(1)
-    cotangent_copies.append(push(rims, near, send_misc.at[0, 5], recv_misc.at[0, 5], (other, lon)))
-    poles = extend(0)
-    polar_part = mul(high, poles) + mul(low, poles)
-    for p in range(pairs):
+    def forward(p, polar_part=None):
         taps = [
             taps_f[kernels * (2 * p + x // COLS) : kernels * (2 * p + x // COLS + 1),
                    x * window : (x + 1) * window]
@@ -358,10 +355,24 @@
         value = mul(taps, ext[0, pl.ds(2 * p * SLOTS, window)])
         if p == 0:
             value = value + jnp.where(north, polar_part, 0.0)
-        if p == pairs - 1:
+        elif p == pairs - 1:
             value = value + jnp.where(north, 0.0, polar_part)
         for h in range(channels // 128):
             sums[h, pl.ds(16 * kernels * p, 16 * kernels)] = value[:, 128 * h : 128 * (h + 1)]
+
+    for copy in field_copies[n - 1 :]:
+        copy.wait()
+    extend_inside(0)
+    for p in range(1, pairs - 1):
+        forward(p)
+    for copy in field_copies[: n - 1]:
+        copy.wait()
+    cotangent_copies = send_field(1)
+    cotangent_copies.append(push(rims, near, send_misc.at[0, 5], recv_misc.at[0, 5], (other, lon)))
+    poles = extend_ends(0)
+    polar_part = mul(high, poles) + mul(low, poles)
+    forward(0, polar_part)
+    forward(pairs - 1, polar_part)
 
     cot = fc[1]
 
@@ -440,7 +451,8 @@
     acc[...] = jnp.zeros_like(acc)
     for copy in cotangent_copies[:-1]:
         copy.wait()
-    poles = extend(1)
+    extend_inside(1)
+    poles = extend_ends(1)
     loads[5].wait()
 
     def per_kernel(k, pole_acc):

time: 40.2 us -> 40.2 us (level)
  no operation moved by 1% of the time
where the time goes in v7:
time: 40.2 us; the launch traced here: 40 us
  Pallas kernels  36.6 us (91%)
  other arithmetic  2.13 us (5%)
  between operations  0.65 us (2%)
  local copies, waits for them, and re-layouts  0.63 us (2%)
    pallas_call x1, Pallas kernels, in_kernel(): pl.pallas_call(functools.partial(fused, n), out_shape=(jax.ShapeDtypeStru...  36.6 us
    reshape x1, other arithmetic, in_kernel(): grad_weights.astype(f32).reshape(kernels // 2, channels, channels)  2.13 us

profile of v7, /device:TPU:0, one launch (start us, length us, event | category | flops | bytes accessed | tf_op | source)
XLA Modules:
  0.0 40.0 jit_solution(7137877346884104810)
XLA Ops:
  0.6 36.6 %shard_map.86 = (bf16[128,256]{1,0:T(8,128)(2,1)}, bf16[1024,256]{1,0:T(8,128)(2,1)}) custom-call(bf16[128,256]{1,0:T(8,128)(2,1)} %bitcast.10, bf16[128,256]{1,0:T(8,128)(2,1)} %bitcast.11, bf16[8,256,256]{2,1,0:T(8,128)(2,1)} %w_hbm.1, bf16[120,16]{1,0:T(8,128)(2,1)} %bitcast.14, s32[16]{0:T(128)} %reach_ref.1, f32[64,128]{1,0:T(8,128)} %bitcast.13, ...), custom_call_target="tpu_custom_call" | custom-call | tf_op jit(solution)/shard_map/pallas_call | solution.py:521
  37.2 0.0 copy-start
  37.2 2.1 %convert.1 = f32[4,256,256]{2,1,0:T(8,128)} convert(bf16[4,256,256]{2,1,0:T(8,128)(2,1)} %bitcast.9) | non-fusion elementwise | flops 262144 | bytes 1572864 | tf_op jit(solution)/shard_map/reshape | solution.py:572
  39.4 0.0 copy-done
  39.4 0.6 %copy.10 = bf16[16,8,256]{2,1,0:T(8,128)(2,1)} copy(bf16[16,8,256]{2,1,0:T(8,128)(2,1)S(1)} %bitcast.12) | data formatting | bytes 131072
Async XLA Ops:
  37.2 2.1 %copy-start = (bf16[128,256]{1,0:T(8,128)(2,1)S(1)}, bf16[128,256]{1,0:T(8,128)(2,1)}, u32[]{:S(2)}) copy-start(bf16[128,256]{1,0:T(8,128)(2,1)} %get-tuple-element.4) | copy-start | bytes 196612
